TPU v7x, 32 devices: a whole 2x2x4 slice. The times are simulated.
32 devices in a mesh: section: 2 (over z_hi), dp: 8 (over y, x, core), shard: 2 (over z_lo).
Axes of the slice: x: 2, y: 2, z: 4 (z_hi: 2, z_lo: 2; z = z_hi * 2 + z_lo), core: 2. Of those that a mesh axis runs over, the one named last changes fastest.
Arguments:
- tokens: bfloat16 [2, 2048, 1536], P(None, 'dp'), may hold values from -6 to 6
- lengths: int32 [2, 8, 4], P(None, 'dp'), may hold values from 1 to 128, 256 in all within a row
- routes: int32 [2, 2, 2048, 4], P('section', None, 'dp'), may hold values from 0 to 7, all different within a row; in each aligned block of 256 rows (0 to 255, 256 to 511, ..., all dimensions but the last counted through in order) at most 256 rows name the same one
- gates: float32 [2, 2, 2048, 4], P('section', None, 'dp'), may hold values from 0.15 to 0.4
- attn_gain: float32 [2, 1536], P('section'), may hold values from 0.5 to 1.5
- q_weight: bfloat16 [2, 1536, 1536], P('section', None, 'shard'), may hold values from -0.15625 to 0.15625
- key_projection: bfloat16 [2, 1536, 256], P('section', None, 'shard'), may hold values from -0.15625 to 0.15625
- value_projection: bfloat16 [2, 1536, 256], P('section', None, 'shard'), may hold values from -0.15625 to 0.15625
- o_weight: bfloat16 [2, 1536, 1536], P('section', None, 'shard'), may hold values from -0.3125 to 0.3125
- mlp_gain: float32 [2, 1536], P('section'), may hold values from 0.5 to 1.5
- expert_gate: bfloat16 [2, 8, 1536, 768], P('section', 'dp', None, 'shard'), may hold values from -0.15625 to 0.15625
- expert_up: bfloat16 [2, 8, 1536, 768], P('section', 'dp', None, 'shard'), may hold values from -0.15625 to 0.15625
- expert_down: bfloat16 [2, 8, 768, 1536], P('section', 'dp', 'shard'), may hold values from -0.4375 to 0.4375
- cotangent: bfloat16 [2, 2048, 1536], P(None, 'dp'), may hold values from -6 to 6
Outputs:
- section_out: bfloat16 [2, 2, 2048, 1536], P('section', None, 'dp', 'shard')
- input_grad: float32 [2, 2, 2048, 1536], P('section', None, 'dp', 'shard')
- attn_gain_grad: float32 [2, 1536], P('section', 'dp')
- q_weight_grad: float32 [2, 1536, 1536], P('section', 'dp', 'shard')
- k_weight_grad: float32 [2, 1536, 256], P('section', 'dp', 'shard')
- v_weight_grad: float32 [2, 1536, 256], P('section', 'dp', 'shard')
- o_weight_grad: float32 [2, 1536, 1536], P('section', 'dp', 'shard')
- mlp_gain_grad: float32 [2, 1536], P('section', 'dp')
- expert_gate_grad: float32 [2, 8, 1536, 768], P('section', 'dp', None, 'shard')
- expert_up_grad: float32 [2, 8, 1536, 768], P('section', 'dp', None, 'shard')
- expert_down_grad: float32 [2, 8, 768, 1536], P('section', 'dp', 'shard')
Inputs may be any that keep to these rules, and one draw needn't show every extreme that they name: `routes`: in each aligned block of 256 rows (one section, micro-batch and index of dp), no expert is named by more than 256 rows, a bound that some block reaches. The 4 lengths of a block sum to 256; the longest is exactly 128.
All inputs are finite; a program needn't handle non-finite values.
Results may differ from a plain program's by a relative error of at most 0.03.
Values may be sent and summed in bfloat16 or wider, within the bound.
No kernel may reach another device: no remote copies, remote signals or barrier semaphores. Data moves between devices by JAX's collectives and lax.ppermute only.
A program may use at most 256 MiB of HBM per device.

v0:
```python
import jax
import jax.numpy as jnp
from jax import lax
from jax.sharding import PartitionSpec as P

HEAD_SIZE = 128


epsilon = 1e-06
masked_value = -1e30


def passed_along(shard, axis, by):
    peers = lax.axis_size(axis)
    pairs = [(i, i + by) for i in range(peers) if 0 <= i + by < peers]
    return lax.ppermute(shard, axis, pairs)


def norm_rows(values, gain_vec):
    factor = lax.rsqrt(jnp.mean(values * values, axis=1, keepdims=True) + epsilon)
    return (values * factor * gain_vec, factor)


def norm_back(values, factor, gain_vec, grad_normed):
    gain_grad = jnp.sum(grad_normed * values * factor, axis=0)
    scaled = grad_normed * gain_vec
    row_inner = jnp.mean(scaled * values, axis=1, keepdims=True)
    return (factor * (scaled - values * factor * factor * row_inner), gain_grad)


def segment_mask(lens_row, tok_rows):
    seq_ends = jnp.cumsum(lens_row)
    position = jnp.arange(tok_rows, dtype=jnp.int32)
    segment = jnp.sum((position[:, None] >= seq_ends[None, :]).astype(jnp.int32), axis=1)
    return (segment[:, None] == segment[None, :]) & (position[None, :] <= position[:, None])


def contract_rows(left_mat, right_mat):
    return lax.dot_general(
        left_mat, right_mat, (((0,), (0,)), ((), ())), preferred_element_type=jnp.float32
    )


def contract_cols(left_mat, right_mat):
    return lax.dot_general(
        left_mat, right_mat, (((1,), (1,)), ((), ())), preferred_element_type=jnp.float32
    )


def slot_tables(route_rows, experts, capacity):
    tok_rows, top_count = route_rows.shape
    flat_route = route_rows.reshape(-1)
    onehot = (flat_route[:, None] == jnp.arange(experts, dtype=jnp.int32)[None, :]).astype(
        jnp.int32
    )
    earlier = jnp.cumsum(onehot, axis=0) - onehot
    slot_index = jnp.sum(earlier * onehot, axis=1)
    target = flat_route * capacity + slot_index
    filler = jnp.full((experts * capacity,), tok_rows * top_count, jnp.int32)
    source = filler.at[target].set(jnp.arange(tok_rows * top_count, dtype=jnp.int32))
    return (target, source)


def expert_rows(rows, w_gate, w_up, w_down):
    sources, slot_count, model_dim = rows.shape
    flat_rows = rows.reshape(sources * slot_count, model_dim)
    gate_out = jnp.dot(flat_rows, w_gate, preferred_element_type=jnp.float32)
    up_out = jnp.dot(flat_rows, w_up, preferred_element_type=jnp.float32)
    activated = (jax.nn.silu(gate_out) * up_out).astype(jnp.bfloat16)
    partial_value = jnp.dot(activated, w_down, preferred_element_type=jnp.float32).astype(
        jnp.bfloat16
    )
    hidden_width = w_gate.shape[1]
    return (
        partial_value.reshape(sources, slot_count, model_dim),
        gate_out.reshape(sources, slot_count, hidden_width),
        up_out.reshape(sources, slot_count, hidden_width),
        rows,
    )


def layer_forward(inputs, lens_row, route_rows, gate_vals, params):
    attn_gain, query_matrix, key_matrix, value_matrix, w_out, mlp_gain, w_gate, w_up, w_down = (
        params
    )
    tok_rows, model_dim = inputs.shape
    normed_one, factor_one = norm_rows(inputs, attn_gain)
    normed_low = normed_one.astype(jnp.bfloat16)
    query_rows = jnp.dot(normed_low, query_matrix, preferred_element_type=jnp.float32).astype(
        jnp.bfloat16
    )
    key_rows = jnp.dot(normed_low, key_matrix, preferred_element_type=jnp.float32).astype(
        jnp.bfloat16
    )
    value_rows = jnp.dot(normed_low, value_matrix, preferred_element_type=jnp.float32).astype(
        jnp.bfloat16
    )
    kv_heads = key_rows.shape[1] // HEAD_SIZE
    query_group_size = query_rows.shape[1] // HEAD_SIZE // kv_heads
    heads_of_query = query_rows.reshape(tok_rows, kv_heads, query_group_size, HEAD_SIZE)
    heads_of_key = key_rows.reshape(tok_rows, kv_heads, HEAD_SIZE)
    heads_of_value = value_rows.reshape(tok_rows, kv_heads, HEAD_SIZE)
    allowed = segment_mask(lens_row, tok_rows)[None, None]
    scores = jnp.where(
        allowed,
        jnp.einsum(
            "qngd,knd->ngqk", heads_of_query, heads_of_key, preferred_element_type=jnp.float32
        )
        * HEAD_SIZE ** (-0.5),
        masked_value,
    )
    row_max = jnp.max(scores, axis=-1, keepdims=True)
    exp_scores = jnp.exp(scores - row_max)
    row_sum = jnp.sum(exp_scores, axis=-1, keepdims=True)
    attn_probs = exp_scores / row_sum
    log_total = row_max + jnp.log(row_sum)
    head_out = jnp.einsum(
        "ngqk,knd->qngd",
        attn_probs.astype(jnp.bfloat16),
        heads_of_value,
        preferred_element_type=jnp.float32,
    )
    head_out = head_out.astype(jnp.bfloat16).reshape(tok_rows, -1)
    attention = lax.psum(contract_cols(head_out, w_out), "shard")
    hidden = inputs + attention
    normed_two, factor_two = norm_rows(hidden, mlp_gain)
    normed_low_two = normed_two.astype(jnp.bfloat16)
    experts = lax.axis_size("dp")
    top_count = route_rows.shape[1]
    capacity = 2 * tok_rows * top_count // experts
    target, source = slot_tables(route_rows, experts, capacity)
    padded = jnp.concatenate([normed_low_two, jnp.zeros((1, model_dim), jnp.bfloat16)], axis=0)
    outgoing = jnp.take(padded, source // top_count, axis=0).reshape(experts, capacity, model_dim)
    partial_rows, gate_out, up_out, rows_in = expert_rows(
        lax.all_to_all(outgoing, "dp", split_axis=0, concat_axis=0, tiled=True),
        w_gate,
        w_up,
        w_down,
    )
    returned = lax.all_to_all(partial_rows, "dp", split_axis=0, concat_axis=0, tiled=True)
    picked = jnp.take(returned.reshape(experts * capacity, model_dim), target, axis=0).reshape(
        tok_rows, top_count, model_dim
    )
    moe_part = jnp.sum(gate_vals[:, :, None] * picked, axis=1)
    mixture = lax.psum(moe_part.astype(jnp.bfloat16), "shard").astype(jnp.float32)
    output = hidden + mixture
    saved_state = (
        inputs,
        factor_one,
        normed_low,
        heads_of_query,
        heads_of_key,
        heads_of_value,
        head_out,
        log_total,
        lens_row,
        hidden,
        factor_two,
        target,
        source,
        gate_out,
        up_out,
        rows_in,
        gate_vals,
    )
    return (output, saved_state)


def layer_backward(saved_state, grad_out, params):
    attn_gain, query_matrix, key_matrix, value_matrix, w_out, mlp_gain, w_gate, w_up, w_down = (
        params
    )
    (
        inputs,
        factor_one,
        normed_low,
        heads_of_query,
        heads_of_key,
        heads_of_value,
        head_out,
        log_total,
        lens_row,
        hidden,
        factor_two,
        target,
        source,
        gate_out,
        up_out,
        rows_in,
        gate_vals,
    ) = saved_state
    tok_rows, model_dim = inputs.shape
    top_count = gate_vals.shape[1]
    experts = lax.axis_size("dp")
    capacity = rows_in.shape[1]
    scaled_rows = (
        (gate_vals[:, :, None] * grad_out[:, None, :])
        .astype(jnp.bfloat16)
        .reshape(tok_rows * top_count, model_dim)
    )
    padded = jnp.concatenate([scaled_rows, jnp.zeros((1, model_dim), jnp.bfloat16)], axis=0)
    outgoing = jnp.take(padded, source, axis=0).reshape(experts, capacity, model_dim)
    arrived = lax.all_to_all(outgoing, "dp", split_axis=0, concat_axis=0, tiled=True)
    grad_rows = arrived.reshape(-1, model_dim)
    hidden_width = gate_out.shape[2]
    flat_gate = gate_out.reshape(-1, hidden_width)
    flat_up = up_out.reshape(-1, hidden_width)
    flat_in = rows_in.reshape(-1, model_dim)
    grad_act = contract_cols(grad_rows, w_down)
    sigmoid_gate = jax.nn.sigmoid(flat_gate)
    silu_gate = flat_gate * sigmoid_gate
    grad_gate = (
        grad_act * flat_up * sigmoid_gate * (1.0 + flat_gate * (1.0 - sigmoid_gate))
    ).astype(jnp.bfloat16)
    grad_up = (grad_act * silu_gate).astype(jnp.bfloat16)
    activated = (silu_gate * flat_up).astype(jnp.bfloat16)
    down_grad = contract_rows(activated, grad_rows)
    gate_grad = contract_rows(flat_in, grad_gate)
    up_grad = contract_rows(flat_in, grad_up)
    grad_in = (contract_cols(grad_gate, w_gate) + contract_cols(grad_up, w_up)).astype(jnp.bfloat16)
    back_rows = lax.all_to_all(
        grad_in.reshape(experts, capacity, model_dim), "dp", split_axis=0, concat_axis=0, tiled=True
    )
    picked = jnp.take(back_rows.reshape(experts * capacity, model_dim), target, axis=0).reshape(
        tok_rows, top_count, model_dim
    )
    grad_normed_two = lax.psum(
        jnp.sum(picked, axis=1, dtype=jnp.float32).astype(jnp.bfloat16), "shard"
    ).astype(jnp.float32)
    grad_hidden_norm, mlp_gain_grad = norm_back(hidden, factor_two, mlp_gain, grad_normed_two)
    grad_hidden = grad_out + grad_hidden_norm
    grad_low = grad_hidden.astype(jnp.bfloat16)
    out_grad = contract_rows(grad_low, head_out)
    kv_heads = heads_of_key.shape[1]
    query_group_size = heads_of_query.shape[2]
    grad_heads = jnp.dot(grad_low, w_out, preferred_element_type=jnp.float32).astype(jnp.bfloat16)
    grad_heads = grad_heads.reshape(tok_rows, kv_heads, query_group_size, HEAD_SIZE)
    allowed = segment_mask(lens_row, tok_rows)[None, None]
    scores = jnp.where(
        allowed,
        jnp.einsum(
            "qngd,knd->ngqk", heads_of_query, heads_of_key, preferred_element_type=jnp.float32
        )
        * HEAD_SIZE ** (-0.5),
        masked_value,
    )
    attn_probs = jnp.exp(scores - log_total)
    grad_probs = jnp.einsum(
        "qngd,knd->ngqk", grad_heads, heads_of_value, preferred_element_type=jnp.float32
    )
    row_inner = jnp.sum(attn_probs * grad_probs, axis=-1, keepdims=True)
    grad_scores = (attn_probs * (grad_probs - row_inner) * HEAD_SIZE ** (-0.5)).astype(jnp.bfloat16)
    query_grad = jnp.einsum(
        "ngqk,knd->qngd", grad_scores, heads_of_key, preferred_element_type=jnp.float32
    )
    query_grad = query_grad.astype(jnp.bfloat16).reshape(tok_rows, -1)
    key_grad = jnp.einsum(
        "ngqk,qngd->knd", grad_scores, heads_of_query, preferred_element_type=jnp.float32
    )
    key_grad = key_grad.astype(jnp.bfloat16).reshape(tok_rows, -1)
    value_grad = jnp.einsum(
        "ngqk,qngd->knd",
        attn_probs.astype(jnp.bfloat16),
        grad_heads,
        preferred_element_type=jnp.float32,
    )
    value_grad = value_grad.astype(jnp.bfloat16).reshape(tok_rows, -1)
    query_w_grad = contract_rows(normed_low, query_grad)
    key_w_grad = contract_rows(normed_low, key_grad)
    value_w_grad = contract_rows(normed_low, value_grad)
    grad_normed_one = (
        contract_cols(query_grad, query_matrix)
        + contract_cols(key_grad, key_matrix)
        + contract_cols(value_grad, value_matrix)
    )
    grad_normed_one = lax.psum(grad_normed_one.astype(jnp.bfloat16), "shard").astype(jnp.float32)
    grad_input_norm, attn_gain_grad = norm_back(inputs, factor_one, attn_gain, grad_normed_one)
    grad_input = grad_hidden + grad_input_norm
    return (
        grad_input,
        (query_w_grad, key_w_grad, value_w_grad, out_grad, attn_gain_grad, mlp_gain_grad),
        (gate_grad, up_grad, down_grad),
    )


def local(
    tokens,
    lengths,
    routes,
    gates,
    attn_gain,
    q_weight,
    key_projection,
    value_projection,
    o_weight,
    mlp_gain,
    expert_gate,
    expert_up,
    expert_down,
    cotangent,
):
    section_index = lax.axis_index("section")
    shard_index = lax.axis_index("shard")
    micro_count = tokens.shape[0]
    tok_rows = tokens.shape[1]
    model_dim = tokens.shape[2]
    half_dim = model_dim // lax.axis_size("shard")
    params = (
        attn_gain[0],
        q_weight[0],
        key_projection[0],
        value_projection[0],
        o_weight[0],
        mlp_gain[0],
        expert_gate[0, 0],
        expert_up[0, 0],
        expert_down[0, 0],
    )
    saved_list = []
    layer_outs = []
    arriving = jnp.zeros((tok_rows, model_dim), jnp.bfloat16)
    for moment in range(micro_count + 1):
        micro_pick = jnp.clip(moment - section_index, 0, micro_count - 1)
        first_input = tokens[min(moment, micro_count - 1)].astype(jnp.float32)
        layer_input = jnp.where(section_index == 0, first_input, arriving.astype(jnp.float32))
        lens_row = lax.dynamic_index_in_dim(lengths[:, 0], micro_pick, 0, keepdims=False)
        route_rows = lax.dynamic_index_in_dim(routes[0], micro_pick, 0, keepdims=False)
        gate_vals = lax.dynamic_index_in_dim(gates[0], micro_pick, 0, keepdims=False)
        result, saved_state = layer_forward(layer_input, lens_row, route_rows, gate_vals, params)
        result_low = result.astype(jnp.bfloat16)
        saved_list.append(saved_state)
        layer_outs.append(result_low)
        if moment < micro_count:
            arriving = passed_along(result_low, "section", 1)
    attn_sums = None
    expert_sums = None
    input_grads = []
    coming = jnp.zeros((tok_rows, model_dim), jnp.bfloat16)
    for moment in range(micro_count + 1):
        if moment < micro_count:
            own_grad = cotangent[micro_count - 1 - moment].astype(jnp.float32)
        else:
            own_grad = jnp.zeros((tok_rows, model_dim), jnp.float32)
        grad_out = jnp.where(section_index == 1, own_grad, coming.astype(jnp.float32))
        grad_input, attn_grads, expert_grads = layer_backward(
            saved_list[micro_count - moment], grad_out, params
        )
        attn_sums = (
            attn_grads if attn_sums is None else jax.tree.map(jnp.add, attn_sums, attn_grads)
        )
        expert_sums = (
            expert_grads
            if expert_sums is None
            else jax.tree.map(jnp.add, expert_sums, expert_grads)
        )
        input_grads.append(grad_input)
        if moment < micro_count:
            coming = passed_along(grad_input.astype(jnp.bfloat16), "section", -1)
    query_sum, key_sum, value_sum, out_sum, gain_one_sum, gain_two_sum = attn_sums
    attn_sums = (
        lax.psum_scatter(
            query_sum.astype(jnp.bfloat16), "dp", scatter_dimension=0, tiled=True
        ).astype(jnp.float32),
        lax.psum_scatter(
            key_sum.astype(jnp.bfloat16), "dp", scatter_dimension=0, tiled=True
        ).astype(jnp.float32),
        lax.psum_scatter(
            value_sum.astype(jnp.bfloat16), "dp", scatter_dimension=0, tiled=True
        ).astype(jnp.float32),
        lax.psum_scatter(
            out_sum.astype(jnp.bfloat16), "dp", scatter_dimension=0, tiled=True
        ).astype(jnp.float32),
        lax.psum_scatter(
            gain_one_sum.astype(jnp.bfloat16), "dp", scatter_dimension=0, tiled=True
        ).astype(jnp.float32),
        lax.psum_scatter(
            gain_two_sum.astype(jnp.bfloat16), "dp", scatter_dimension=0, tiled=True
        ).astype(jnp.float32),
    )
    section_rows = jnp.stack(
        [
            jnp.where(section_index == 0, layer_outs[micro], layer_outs[micro + 1])
            for micro in range(micro_count)
        ]
    )
    grad_rows = jnp.stack(
        [
            jnp.where(
                section_index == 0,
                input_grads[micro_count - micro],
                input_grads[micro_count - micro - 1],
            )
            for micro in range(micro_count)
        ]
    )
    section_out = lax.dynamic_slice_in_dim(section_rows, shard_index * half_dim, half_dim, 2)[None]
    input_grad = lax.dynamic_slice_in_dim(grad_rows, shard_index * half_dim, half_dim, 2)[None]
    query_total, key_total, value_total, out_total, gain_one_total, gain_two_total = attn_sums
    gate_total, up_total, down_total = expert_sums
    return (
        section_out,
        input_grad,
        gain_one_total[None],
        query_total[None],
        key_total[None],
        value_total[None],
        out_total[None],
        gain_two_total[None],
        gate_total[None, None],
        up_total[None, None],
        down_total[None, None],
    )


def solution(mesh):
    in_specs = (
        P(None, "dp", None),
        P(None, "dp", None),
        P("section", None, "dp", None),
        P("section", None, "dp", None),
        P("section", None),
        P("section", None, "shard"),
        P("section", None, "shard"),
        P("section", None, "shard"),
        P("section", None, "shard"),
        P("section", None),
        P("section", "dp", None, "shard"),
        P("section", "dp", None, "shard"),
        P("section", "dp", "shard", None),
        P(None, "dp", None),
    )
    out_specs = (
        P("section", None, "dp", "shard"),
        P("section", None, "dp", "shard"),
        P("section", "dp"),
        P("section", "dp", "shard"),
        P("section", "dp", "shard"),
        P("section", "dp", "shard"),
        P("section", "dp", "shard"),
        P("section", "dp"),
        P("section", "dp", None, "shard"),
        P("section", "dp", None, "shard"),
        P("section", "dp", "shard", None),
    )
    return jax.shard_map(local, mesh=mesh, in_specs=in_specs, out_specs=out_specs, check_vma=False)
```

profile of v0, /device:TPU:0, one launch (start us, length us, event | category | flops | bytes accessed | tf_op | source)
XLA Modules:
  0.0 2151.9 jit_solution(10315773356537378382)
XLA Ops:
  30.4 44.6 %all-reduce.22.cloned.1.call-done = f32[256,1536]{1,0:T(8,128)} async-done(((f32[256,1536]{1,0:T(8,128)}), f32[256,1536]{1,0:T(8,128)}) %all-reduce.22.cloned.1.call-update) | async-done | bytes 1572880 | tf_op jit(solution)/shard_map/psum | solution.py:124
  92.4 75.3 %all_to_all.60 = bf16[8,256,1536]{2,1,0:T(8,128)(2,1)S(1)} all-to-all(bf16[8,256,1536]{2,1,0:T(8,128)(2,1)S(1)} %bitcast.642), channel_id=1, replica_groups=mesh['section'=2,'dp'=8,'shard'=2] {'dp'}, dimensions={0} | all-to-all | bytes 12582912 | tf_op jit(solution)/shard_map/all_to_all | solution.py:135
  187.9 70.5 %all-to-all-done.1 = bf16[8,256,1536]{2,1,0:T(8,128)(2,1)} async-done(((bf16[8,256,1536]{2,1,0:T(8,128)(2,1)}), bf16[8,256,1536]{2,1,0:T(8,128)(2,1)}, u32[]{:S(2)}, u32[]{:S(2)}) %all-to-all-start.1) | async-done | bytes 6291488 | tf_op jit(solution)/shard_map/all_to_all | solution.py:140
  293.2 30.3 %all-reduce.24.cloned.1.call-done = bf16[256,1536]{1,0:T(8,128)(2,1)} async-done(((bf16[256,1536]{1,0:T(8,128)(2,1)}), bf16[256,1536]{1,0:T(8,128)(2,1)}) %all-reduce.24.cloned.1.call-update) | async-done | bytes 786448 | tf_op jit(solution)/shard_map/psum | solution.py:145
  370.9 59.4 %all-reduce.26.cloned.1.call-done = f32[256,1536]{1,0:T(8,128)} async-done(((f32[256,1536]{1,0:T(8,128)}), f32[256,1536]{1,0:T(8,128)}) %all-reduce.26.cloned.1.call-update) | async-done | bytes 1572880 | tf_op jit(solution)/shard_map/psum | solution.py:124
  447.8 75.3 %all_to_all.61 = bf16[8,256,1536]{2,1,0:T(8,128)(2,1)S(1)} all-to-all(bf16[8,256,1536]{2,1,0:T(8,128)(2,1)S(1)} %bitcast.643), channel_id=1, replica_groups=mesh['section'=2,'dp'=8,'shard'=2] {'dp'}, dimensions={0} | all-to-all | bytes 12582912 | tf_op jit(solution)/shard_map/all_to_all | solution.py:135
  542.6 71.1 %all-to-all-done.3 = bf16[8,256,1536]{2,1,0:T(8,128)(2,1)} async-done(((bf16[8,256,1536]{2,1,0:T(8,128)(2,1)}), bf16[8,256,1536]{2,1,0:T(8,128)(2,1)}, u32[]{:S(2)}, u32[]{:S(2)}) %all-to-all-start.3) | async-done | bytes 6291488 | tf_op jit(solution)/shard_map/all_to_all | solution.py:140
  645.6 33.2 %all-reduce.28.cloned.1.call-done = bf16[256,1536]{1,0:T(8,128)(2,1)} async-done(((bf16[256,1536]{1,0:T(8,128)(2,1)}), bf16[256,1536]{1,0:T(8,128)(2,1)}) %all-reduce.28.cloned.1.call-update) | async-done | bytes 786448 | tf_op jit(solution)/shard_map/psum | solution.py:145
  720.6 65.4 %all-reduce.30.cloned.1.call-done = f32[256,1536]{1,0:T(8,128)} async-done(((f32[256,1536]{1,0:T(8,128)}), f32[256,1536]{1,0:T(8,128)}) %all-reduce.30.cloned.1.call-update) | async-done | bytes 1572880 | tf_op jit(solution)/shard_map/psum | solution.py:124
  849.9 31.9 %all-to-all-done.4 = bf16[8,256,1536]{2,1,0:T(8,128)(2,1)} async-done(((bf16[8,256,1536]{2,1,0:T(8,128)(2,1)}), bf16[8,256,1536]{2,1,0:T(8,128)(2,1)}, u32[]{:S(2)}, u32[]{:S(2)}) %all-to-all-start.4) | async-done | bytes 6291488 | tf_op jit(solution)/shard_map/all_to_all | solution.py:135
  902.8 55.5 %all-to-all-done.6 = bf16[8,256,1536]{2,1,0:T(8,128)(2,1)} async-done(((bf16[8,256,1536]{2,1,0:T(8,128)(2,1)}), bf16[8,256,1536]{2,1,0:T(8,128)(2,1)}, u32[]{:S(2)}, u32[]{:S(2)}) %all-to-all-start.6) | async-done | bytes 6291488 | tf_op jit(solution)/shard_map/all_to_all | solution.py:203
  990.5 60.9 %all-to-all-done.5 = bf16[8,256,1536]{2,1,0:T(8,128)(2,1)} async-done(((bf16[8,256,1536]{2,1,0:T(8,128)(2,1)}), bf16[8,256,1536]{2,1,0:T(8,128)(2,1)}, u32[]{:S(2)}, u32[]{:S(2)}) %all-to-all-start.5) | async-done | bytes 6291488 | tf_op jit(solution)/shard_map/all_to_all | solution.py:140
  1067.3 60.6 %all-to-all-done.7 = bf16[8,256,1536]{2,1,0:T(8,128)(2,1)} async-done(((bf16[8,256,1536]{2,1,0:T(8,128)(2,1)}), bf16[8,256,1536]{2,1,0:T(8,128)(2,1)}, u32[]{:S(2)}, u32[]{:S(2)}) %all-to-all-start.7) | async-done | bytes 6291488 | tf_op jit(solution)/shard_map/all_to_all | solution.py:221
  1158.1 32.7 %all-reduce.32.cloned.1.call-done = bf16[256,1536]{1,0:T(8,128)(2,1)} async-done(((bf16[256,1536]{1,0:T(8,128)(2,1)}), bf16[256,1536]{1,0:T(8,128)(2,1)}) %all-reduce.32.cloned.1.call-update) | async-done | bytes 786448 | tf_op jit(solution)/shard_map/psum | solution.py:227
  1206.0 35.0 %all-reduce.34.cloned.1.call-done = bf16[256,1536]{1,0:T(8,128)(2,1)} async-done(((bf16[256,1536]{1,0:T(8,128)(2,1)}), bf16[256,1536]{1,0:T(8,128)(2,1)}) %all-reduce.34.cloned.1.call-update) | async-done | bytes 786448 | tf_op jit(solution)/shard_map/psum | solution.py:276
  1251.5 34.7 %collective-permute-done.2 = bf16[256,1536]{1,0:T(8,128)(2,1)S(1)} collective-permute-done((bf16[256,1536]{1,0:T(8,128)(2,1)}, bf16[256,1536]{1,0:T(8,128)(2,1)S(1)}, u32[]{:S(2)}, u32[]{:S(2)}) %collective-permute-start.2) | collective-permute-done | bytes 786464 | tf_op jit(solution)/shard_map/ppermute | solution.py:16
  1325.0 75.5 %all_to_all.62 = bf16[8,256,1536]{2,1,0:T(8,128)(2,1)S(1)} all-to-all(bf16[8,256,1536]{2,1,0:T(8,128)(2,1)S(1)} %bitcast.644), channel_id=1, replica_groups=mesh['section'=2,'dp'=8,'shard'=2] {'dp'}, dimensions={0} | all-to-all | bytes 12582912 | tf_op jit(solution)/shard_map/all_to_all | solution.py:203
  1416.3 77.0 %all_to_all.63 = bf16[8,256,1536]{2,1,0:T(8,128)(2,1)} all-to-all(bf16[8,256,1536]{2,1,0:T(8,128)(2,1)} %bitcast.646), channel_id=1, replica_groups=mesh['section'=2,'dp'=8,'shard'=2] {'dp'}, dimensions={0} | all-to-all | bytes 12582912 | tf_op jit(solution)/shard_map/all_to_all | solution.py:221
  1522.0 30.3 %all-reduce.36.cloned.1.call-done = bf16[256,1536]{1,0:T(8,128)(2,1)} async-done(((bf16[256,1536]{1,0:T(8,128)(2,1)}), bf16[256,1536]{1,0:T(8,128)(2,1)}) %all-reduce.36.cloned.1.call-update) | async-done | bytes 786448 | tf_op jit(solution)/shard_map/psum | solution.py:227
  1567.4 35.0 %all-reduce.38.cloned.1.call-done = bf16[256,1536]{1,0:T(8,128)(2,1)} async-done(((bf16[256,1536]{1,0:T(8,128)(2,1)}), bf16[256,1536]{1,0:T(8,128)(2,1)}) %all-reduce.38.cloned.1.call-update) | async-done | bytes 786448 | tf_op jit(solution)/shard_map/psum | solution.py:276
  1614.9 34.6 %collective-permute-done.3 = bf16[256,1536]{1,0:T(8,128)(2,1)S(1)} collective-permute-done((bf16[256,1536]{1,0:T(8,128)(2,1)}, bf16[256,1536]{1,0:T(8,128)(2,1)S(1)}, u32[]{:S(2)}, u32[]{:S(2)}) %collective-permute-start.3) | collective-permute-done | bytes 786464 | tf_op jit(solution)/shard_map/ppermute | solution.py:16
  1685.9 75.5 %all_to_all.64 = bf16[8,256,1536]{2,1,0:T(8,128)(2,1)S(1)} all-to-all(bf16[8,256,1536]{2,1,0:T(8,128)(2,1)S(1)} %bitcast.645), channel_id=1, replica_groups=mesh['section'=2,'dp'=8,'shard'=2] {'dp'}, dimensions={0} | all-to-all | bytes 12582912 | tf_op jit(solution)/shard_map/all_to_all | solution.py:203
  1997.6 53.8 %all-reduce.42.cloned.1.call-done = (bf16[256,1536]{1,0:T(8,128)(2,1)}, bf16[256,1536]{1,0:T(8,128)(2,1)}) async-done(((bf16[256,1536]{1,0:T(8,128)(2,1)}, bf16[256,1536]{1,0:T(8,128)(2,1)}), (bf16[256,1536]{1,0:T(8,128)(2,1)}, bf16[256,1536]{1,0:T(8,128)(2,1)})) %all-reduce.42.cloned.1.call-update) | async-done | bytes 1572880 | tf_op jit(solution)/shard_map/psum | solution.py:145
  2099.2 43.9 %reduce-scatter.5.cloned.1.call-done = bf16[192,768]{1,0:T(8,128)(2,1)} async-done(((bf16[1536,768]{1,0:T(8,128)(2,1)}), bf16[192,768]{1,0:T(8,128)(2,1)}) %reduce-scatter.5.cloned.1.call-update) | async-done | bytes 294928 | tf_op jit(solution)/shard_map/reduce_scatter | solution.py:361
  (751 shorter events, 872.1 us)
Async XLA Ops:
  7.2 67.8 %all-reduce.22.cloned.1.call-start = ((), (), s32[]{:S(2)}) async-start(), calls=%async_computation.16 | async-start | bytes 3145728 | tf_op jit(solution)/shard_map/psum | solution.py:124
  181.8 76.6 %all-to-all-start.1 = ((bf16[8,256,1536]{2,1,0:T(8,128)(2,1)}), bf16[8,256,1536]{2,1,0:T(8,128)(2,1)}, u32[]{:S(2)}, u32[]{:S(2)}) async-start(bf16[8,256,1536]{2,1,0:T(8,128)(2,1)} %bitcast.657), calls=%async_computation.1 | async-start | bytes 12582912 | tf_op jit(solution)/shard_map/all_to_all | solution.py:140
  186.7 136.7 %all-reduce.24.cloned.1.call-start = ((), (), s32[]{:S(2)}) async-start(), calls=%async_computation.17 | async-start | bytes 1572864 | tf_op jit(solution)/shard_map/psum | solution.py:145
  290.2 140.1 %all-reduce.26.cloned.1.call-start = ((), (), s32[]{:S(2)}) async-start(), calls=%async_computation.18 | async-start | bytes 3145728 | tf_op jit(solution)/shard_map/psum | solution.py:124
  537.2 76.5 %all-to-all-start.3 = ((bf16[8,256,1536]{2,1,0:T(8,128)(2,1)}), bf16[8,256,1536]{2,1,0:T(8,128)(2,1)}, u32[]{:S(2)}, u32[]{:S(2)}) async-start(bf16[8,256,1536]{2,1,0:T(8,128)(2,1)} %bitcast.658), calls=%async_computation.3 | async-start | bytes 12582912 | tf_op jit(solution)/shard_map/all_to_all | solution.py:140
  542.1 136.7 %all-reduce.28.cloned.1.call-start = ((), (), s32[]{:S(2)}) async-start(), calls=%async_computation.19 | async-start | bytes 1572864 | tf_op jit(solution)/shard_map/psum | solution.py:145
  645.5 140.4 %all-reduce.30.cloned.1.call-start = ((), (), s32[]{:S(2)}) async-start(), calls=%async_computation.20 | async-start | bytes 3145728 | tf_op jit(solution)/shard_map/psum | solution.py:124
  805.3 76.5 %all-to-all-start.4 = ((bf16[8,256,1536]{2,1,0:T(8,128)(2,1)}), bf16[8,256,1536]{2,1,0:T(8,128)(2,1)}, u32[]{:S(2)}, u32[]{:S(2)}) async-start(bf16[8,256,1536]{2,1,0:T(8,128)(2,1)} %bitcast.639), calls=%async_computation.4 | async-start | bytes 12582912 | tf_op jit(solution)/shard_map/all_to_all | solution.py:135
  881.8 76.5 %all-to-all-start.6 = ((bf16[8,256,1536]{2,1,0:T(8,128)(2,1)}), bf16[8,256,1536]{2,1,0:T(8,128)(2,1)}, u32[]{:S(2)}, u32[]{:S(2)}) async-start(bf16[8,256,1536]{2,1,0:T(8,128)(2,1)} %bitcast.641), calls=%async_computation.6 | async-start | bytes 12582912 | tf_op jit(solution)/shard_map/all_to_all | solution.py:203
  974.8 76.6 %all-to-all-start.5 = ((bf16[8,256,1536]{2,1,0:T(8,128)(2,1)}), bf16[8,256,1536]{2,1,0:T(8,128)(2,1)}, u32[]{:S(2)}, u32[]{:S(2)}) async-start(bf16[8,256,1536]{2,1,0:T(8,128)(2,1)} %bitcast.659), calls=%async_computation.5 | async-start | bytes 12582912 | tf_op jit(solution)/shard_map/all_to_all | solution.py:140
  1051.4 76.5 %all-to-all-start.7 = ((bf16[8,256,1536]{2,1,0:T(8,128)(2,1)}), bf16[8,256,1536]{2,1,0:T(8,128)(2,1)}, u32[]{:S(2)}, u32[]{:S(2)}) async-start(bf16[8,256,1536]{2,1,0:T(8,128)(2,1)} %bitcast.640), calls=%async_computation.7 | async-start | bytes 12582912 | tf_op jit(solution)/shard_map/all_to_all | solution.py:221
  1056.3 134.5 %all-reduce.32.cloned.1.call-start = ((), (), s32[]{:S(2)}) async-start(), calls=%async_computation.21 | async-start | bytes 1572864 | tf_op jit(solution)/shard_map/psum | solution.py:227
  1157.6 83.4 %all-reduce.34.cloned.1.call-start = ((), (), s32[]{:S(2)}) async-start(), calls=%async_computation.22 | async-start | bytes 1572864 | tf_op jit(solution)/shard_map/psum | solution.py:276
  1205.9 346.4 %all-reduce.36.cloned.1.call-start = ((), (), s32[]{:S(2)}) async-start(), calls=%async_computation.23 | async-start | bytes 1572864 | tf_op jit(solution)/shard_map/psum | solution.py:227
  1247.2 39.0 %collective-permute-start.2 = (bf16[256,1536]{1,0:T(8,128)(2,1)}, bf16[256,1536]{1,0:T(8,128)(2,1)S(1)}, u32[]{:S(2)}, u32[]{:S(2)}) collective-permute-start(bf16[256,1536]{1,0:T(8,128)(2,1)} %get-tuple-element.32), channel_id=1, source_target_pairs={{16,0},{17,1},{18,2},{19,3},{20,4},{21,5},{22,6},{23,7},{24,8},{25... | collective-permute-start | bytes 2359304 | tf_op jit(solution)/shard_map/ppermute | solution.py:16
  1520.9 81.5 %all-reduce.38.cloned.1.call-start = ((), (), s32[]{:S(2)}) async-start(), calls=%async_computation.24 | async-start | bytes 1572864 | tf_op jit(solution)/shard_map/psum | solution.py:276
  1610.5 39.0 %collective-permute-start.3 = (bf16[256,1536]{1,0:T(8,128)(2,1)}, bf16[256,1536]{1,0:T(8,128)(2,1)S(1)}, u32[]{:S(2)}, u32[]{:S(2)}) collective-permute-start(bf16[256,1536]{1,0:T(8,128)(2,1)} %convert_element_type.561), channel_id=1, source_target_pairs={{16,0},{17,1},{18,2},{19,3},{20,4},{21,5},{22,6},{23,7},{24,8},{25... | collective-permute-start | bytes 2359304 | tf_op jit(solution)/shard_map/ppermute | solution.py:16
  1777.5 76.5 %all-to-all-start.11 = ((bf16[8,256,1536]{2,1,0:T(8,128)(2,1)}), bf16[8,256,1536]{2,1,0:T(8,128)(2,1)}, u32[]{:S(2)}, u32[]{:S(2)}) async-start(bf16[8,256,1536]{2,1,0:T(8,128)(2,1)} %bitcast.638), calls=%async_computation.11 | async-start | bytes 12582912 | tf_op jit(solution)/shard_map/all_to_all | solution.py:221
  1782.4 130.9 %all-reduce.40.cloned.1.call-start = ((), (), s32[]{:S(2)}) async-start(), calls=%async_computation.25 | async-start | bytes 1572864 | tf_op jit(solution)/shard_map/psum | solution.py:227
  1881.9 110.8 %reduce-scatter.9.cloned.1.call-start = ((), (), s32[]{:S(2)}) async-start(), calls=%async_computation.28 | async-start | bytes 442368 | tf_op jit(solution)/shard_map/reduce_scatter | solution.py:367
  1925.4 70.7 %reduce-scatter.7.cloned.1.call-start = ((), (), s32[]{:S(2)}) async-start(), calls=%async_computation.27 | async-start | bytes 442368 | tf_op jit(solution)/shard_map/reduce_scatter | solution.py:364
  1935.8 115.5 %all-reduce.42.cloned.1.call-start = ((), (), s32[]{:S(2)}) async-start(), calls=%async_computation.30 | async-start | bytes 3145728 | tf_op jit(solution)/shard_map/psum | solution.py:145
  1939.1 158.3 %reduce-scatter.11.cloned.1.call-start = ((), (), s32[]{:S(2)}) async-start(), calls=%async_computation.29 | async-start | bytes 2654208 | tf_op jit(solution)/shard_map/reduce_scatter | solution.py:370
  1953.6 189.6 %reduce-scatter.5.cloned.1.call-start = ((), (), s32[]{:S(2)}) async-start(), calls=%async_computation.26 | async-start | bytes 2654208 | tf_op jit(solution)/shard_map/reduce_scatter | solution.py:361
  (214 other events, 2426.7 us)
Sparse Core Ops, SparseCore 0:
  20.2 54.7 all-reduce.21
  290.3 33.1 all-reduce.23
  360.6 69.6 all-reduce.25
  645.7 33.1 all-reduce.27
  716.2 69.7 all-reduce.29
  1157.7 33.1 all-reduce.31
  1206.1 34.8 all-reduce.33
  1521.0 31.2 all-reduce.35
  1567.5 34.8 all-reduce.37
  1882.0 31.2 all-reduce.39
  1925.5 33.7 reduce-scatter.8
  1962.3 33.7 reduce-scatter.6
  1999.1 52.2 all-reduce.41
  2054.9 42.4 reduce-scatter.10
  2100.6 42.4 reduce-scatter.4
where the time goes:
time: 2160 us; the launch traced here: 2150 us
  waiting for transfers between devices  984 us (46%)
  blocking collectives  393 us (18%)
  local copies, waits for them, and re-layouts  281 us (13%)
  matrix products  237 us (11%)
  other arithmetic  191 us (9%)
  starting transfers between devices  48.5 us (2%)
    all_to_all x3, waiting for transfers between devices, layer_forward(): lax.all_to_all(partial_rows, 'dp', split_axis=0, concat_axis=0, tiled=True)  203 us
    psum x3, waiting for transfers between devices, layer_forward(): attention = lax.psum(contract_cols(head_out, w_out), 'shard')  169 us
    all_to_all x2, blocking collectives, layer_backward(): lax.all_to_all(outgoing, 'dp', split_axis=0, concat_axis=0, tiled=True)  151 us
    all_to_all x2, blocking collectives, layer_forward(): lax.all_to_all(outgoing, 'dp', split_axis=0, concat_axis=0, tiled=True)  151 us
    psum x3, waiting for transfers between devices, layer_forward(): lax.psum(moe_part.astype(jnp.bfloat16), 'shard').astype(jnp.float32)  117 us
    ppermute x4, waiting for transfers between devices, passed_along(): return lax.ppermute(shard, axis, pairs)  96.4 us
    psum x3, waiting for transfers between devices, layer_backward(): lax.psum(jnp.sum(picked, axis=1, dtype=jnp.float32).astype(jnp.bfloat16),...  90.3 us
    dot_general x21, matrix products, contract_rows(): lax.dot_general(left_mat, right_mat, (((0,), (0,)), ((), ())), preferred_...  87.7 us
  transfers between devices with their start and end apart: 26, of which 25 were waited for; matrix products, arithmetic and copies ran while one was open for 11% of the time, Pallas kernels for 0%

commit v1 on v0

v1 whole, which is shorter than its diff:
```python
import jax
import jax.numpy as jnp
import numpy as np
from jax import lax
from jax.sharding import PartitionSpec as P

HEAD_SIZE = 128
epsilon = 1e-06
masked_value = -1e30
bf16 = jnp.bfloat16
f32 = jnp.float32


def wide(a):
    return a.astype(f32)


def dot_nn(a, b):
    return lax.dot_general(a, b, (((1,), (0,)), ((), ())), preferred_element_type=f32)


def dot_nt(a, b):
    return lax.dot_general(a, b, (((1,), (1,)), ((), ())), preferred_element_type=f32)


def dot_tn(a, b):
    return lax.dot_general(a, b, (((0,), (0,)), ((), ())), preferred_element_type=f32)


class Cube:
    def __init__(self):
        peers = lax.axis_size("dp")
        bits = [1 << i for i in range(peers.bit_length() - 1)]
        rest = bits[1:]
        self.core = ("dp", bits[0])
        self.x = ("dp", rest[0])
        self.y = ("dp", rest[len(rest) // 2])
        self.z = ("shard", 1)
        self.extra = [("dp", b) for b in rest if b not in (self.x[1], self.y[1])]
        inner = [0]
        for _, bit in self.extra:
            inner = inner + [m | bit for m in inner]
        self.inner = np.array(inner)
        x, y = self.x[1], self.y[1]
        self.near = [(0, 0), (x, 0), (y, 0), (0, 1)]
        self.far = [(x | y, 0), (y, 1), (x, 1), (x | y, 1)]

    def mate(self, group):
        return [(m | self.core[1], s) for m, s in group]


def swap(value, direction):
    axis, bit = direction
    return lax.ppermute(value, axis, [(i, i ^ bit) for i in range(lax.axis_size(axis))])


def thirds(rows):
    step = -(-rows // 48) * 16
    return [(0, step), (step, 2 * step), (2 * step, rows)]


def gather_rows(cube, own):
    for direction in cube.extra:
        own = jnp.concatenate([own, swap(own, direction)], axis=0)
    rx, ry, rz = swap(own, cube.x), swap(own, cube.y), swap(own, cube.z)
    own_mate = swap(own, cube.core)
    rxy, ryz, rzx = swap(rx, cube.y), swap(ry, cube.z), swap(rz, cube.x)
    near_mate = swap(jnp.concatenate([rx, ry, rz], axis=0), cube.core)
    cuts = thirds(own.shape[0])
    last = [
        swap(block[lo:hi], direction)
        for block, direction, (lo, hi) in zip((rxy, ryz, rzx), (cube.z, cube.x, cube.y), cuts)
    ]
    far_mate = swap(jnp.concatenate([rxy, ryz, rzx], axis=0), cube.core)
    rxyz = jnp.concatenate(last, axis=0)
    last_mate = swap(rxyz, cube.core)
    near = [own, rx, ry, rz, own_mate, near_mate]
    far = [rxy, ryz, rzx, rxyz, far_mate, last_mate]
    return near, far


def low_sum(*terms):
    return sum(wide(t) for t in terms).astype(bf16)


def reduce_rows(cube, near, near_mate, far, far_mate):
    rows = near.shape[0] // 4
    far_in = swap(far_mate, cube.core)
    near_in = swap(near_mate, cube.core)
    far_sum = low_sum(far, far_in)
    cuts = thirds(rows)
    sent = far_sum[3 * rows :]
    directions = (cube.z, cube.x, cube.y)
    arrived = [swap(sent[lo:hi], d) for d, (lo, hi) in zip(directions, cuts)]
    middle = []
    for i, (lo, hi) in enumerate(cuts):
        block = far_sum[i * rows : (i + 1) * rows]
        middle.append(
            low_sum(block, jnp.pad(arrived[i], ((lo, rows - hi), (0, 0))))
        )
    back = [swap(middle[0], cube.y), swap(middle[1], cube.z), swap(middle[2], cube.x)]
    outer = [
        low_sum(near[i * rows : (i + 1) * rows], near_in[i * rows : (i + 1) * rows], back[i - 1])
        for i in (1, 2, 3)
    ]
    ends = [swap(t, d) for t, d in zip(outer, (cube.x, cube.y, cube.z))]
    total = wide(near[:rows]) + wide(near_in[:rows]) + wide(ends[0]) + wide(ends[1]) + wide(ends[2])
    for direction in reversed(cube.extra):
        half = total.shape[0] // 2
        total = total[:half] + wide(swap(total[half:].astype(bf16), direction))
    return total


def norm_factor(values):
    return lax.rsqrt(jnp.mean(values * values, axis=1, keepdims=True) + epsilon)


def norm_back(values, factor, gain, grad):
    gain_grad = jnp.sum(grad * values * factor, axis=0, keepdims=True)
    scaled = grad * gain
    inner = jnp.mean(scaled * values, axis=1, keepdims=True)
    return factor * (scaled - values * factor * factor * inner), gain_grad


def stack_heads(rows):
    return jnp.concatenate(
        [rows[:, i : i + HEAD_SIZE] for i in range(0, rows.shape[1], HEAD_SIZE)], axis=0
    )


def spread_heads(stacked, rows):
    return jnp.concatenate(
        [stacked[i : i + rows] for i in range(0, stacked.shape[0], rows)], axis=1
    )


def head_probs(query, key, allowed):
    scores = jnp.where(allowed > 0.0, dot_nt(query, key) * HEAD_SIZE ** (-0.5), masked_value)
    exp_scores = jnp.exp(scores - jnp.max(scores, axis=1, keepdims=True))
    return exp_scores / jnp.sum(exp_scores, axis=1, keepdims=True)


def attention_forward(inputs, allowed, attn_gain, mlp_gain, qkv_w, out_w):
    rows = inputs.shape[0]
    normed = (inputs * norm_factor(inputs) * attn_gain).astype(bf16)
    hidden = inputs
    projected, heads = [], []
    for w, w_out in zip(qkv_w, out_w):
        qkv = dot_nn(normed, w).astype(bf16)
        width = qkv.shape[1] - 2 * HEAD_SIZE
        query = stack_heads(qkv[:, :width])
        key, value = qkv[:, width : width + HEAD_SIZE], qkv[:, width + HEAD_SIZE :]
        tiled = jnp.concatenate([allowed] * (width // HEAD_SIZE), axis=0)
        probs = head_probs(query, key, tiled).astype(bf16)
        head_out = spread_heads(dot_nn(probs, value).astype(bf16), rows)
        hidden = hidden + dot_nt(head_out, w_out)
        projected.append(qkv)
        heads.append(head_out)
    normed_two = (hidden * norm_factor(hidden) * mlp_gain).astype(bf16)
    return hidden, normed_two, projected, heads


def attention_backward(grad, grad_two, inputs, hidden, allowed, attn_gain, mlp_gain, projected, qkv_w, out_w):
    rows = inputs.shape[0]
    normed = (inputs * norm_factor(inputs) * attn_gain).astype(bf16)
    back, mlp_gain_grad = norm_back(hidden, norm_factor(hidden), mlp_gain, grad_two)
    grad_hidden = grad + back
    grad_low = grad_hidden.astype(bf16)
    grad_normed = 0.0
    grads = []
    for qkv, w, w_out in zip(projected, qkv_w, out_w):
        width = qkv.shape[1] - 2 * HEAD_SIZE
        grad_heads = stack_heads(dot_nn(grad_low, w_out).astype(bf16))
        query = stack_heads(qkv[:, :width])
        key, value = qkv[:, width : width + HEAD_SIZE], qkv[:, width + HEAD_SIZE :]
        tiled = jnp.concatenate([allowed] * (width // HEAD_SIZE), axis=0)
        probs = head_probs(query, key, tiled)
        grad_probs = dot_nt(grad_heads, value)
        inner = jnp.sum(probs * grad_probs, axis=1, keepdims=True)
        grad_scores = (probs * (grad_probs - inner) * HEAD_SIZE ** (-0.5)).astype(bf16)
        grad_query = spread_heads(dot_nn(grad_scores, key).astype(bf16), rows)
        grad_key = dot_tn(grad_scores, query).astype(bf16)
        grad_value = dot_tn(probs.astype(bf16), grad_heads).astype(bf16)
        grad_qkv = jnp.concatenate([grad_query, grad_key, grad_value], axis=1)
        grad_normed = grad_normed + dot_nt(grad_qkv, w)
        grads.append(grad_qkv)
    back, attn_gain_grad = norm_back(inputs, norm_factor(inputs), attn_gain, grad_normed)
    return grad_hidden + back, grad_low, normed, grads, attn_gain_grad, mlp_gain_grad


def expert_forward(pieces, gate_col, w_gate, w_up, w_down):
    rows = jnp.concatenate(pieces, axis=0)
    gate_out = dot_nn(rows, w_gate)
    up_out = dot_nn(rows, w_up)
    act = (gate_out / (1.0 + jnp.exp(-gate_out)) * up_out).astype(bf16)
    part = dot_nn(act, w_down)
    part = (part if gate_col is None else gate_col * part).astype(bf16)
    return part, (rows, gate_out.astype(bf16), up_out.astype(bf16))


def expert_backward(pieces, gate_col, saved, w_gate, w_up, w_down):
    rows, gate_low, up_low = saved
    gate_out, up_out = wide(gate_low), wide(up_low)
    grad_rows = jnp.concatenate(pieces, axis=0)
    if gate_col is not None:
        grad_rows = (gate_col * wide(grad_rows)).astype(bf16)
    grad_act = dot_nt(grad_rows, w_down)
    sig = 1.0 / (1.0 + jnp.exp(-gate_out))
    silu = gate_out * sig
    grad_gate = (grad_act * up_out * sig * (1.0 + gate_out * (1.0 - sig))).astype(bf16)
    grad_up = (grad_act * silu).astype(bf16)
    act = (silu * up_out).astype(bf16)
    grad_in = (dot_nt(grad_gate, w_gate) + dot_nt(grad_up, w_up)).astype(bf16)
    weights = (dot_tn(rows, grad_gate), dot_tn(rows, grad_up), dot_tn(act, grad_rows))
    return grad_in, weights


def halves(array):
    half = array.shape[0] // 2
    return array[:half], array[half:]


class Blocks:
    def __init__(self, cube, routes, gates, weights):
        self.cube, self.weights = cube, weights
        me, shard = lax.axis_index("dp"), lax.axis_index("shard")
        rows = routes.shape[1] // lax.axis_size("shard")
        numbers = jnp.arange(lax.axis_size("dp"), dtype=jnp.int32)
        table = jnp.sum(
            jnp.where(routes[:, :rows, :, None] == numbers, gates[:, :rows, :, None], 0.0), axis=2
        )
        everyone = lax.all_gather(table, ("dp", "shard"), axis=0)
        column = lax.dynamic_index_in_dim(everyone, me, 3, keepdims=False)

        def ordered(group):
            order = [(me ^ (m ^ cube.inner)) * lax.axis_size("shard") + (shard ^ s) for m, s in group]
            weighed = jnp.take(column, jnp.concatenate(order), axis=0)
            return [weighed[:, m].reshape(-1, 1) for m in range(routes.shape[0])]

        near = ordered(cube.near + cube.mate(cube.near))
        far = ordered(cube.far + cube.mate(cube.far))
        self.tables = list(zip(near, far))

    def forward(self, own, table):
        results, saved = [], []
        for pieces, column in zip(gather_rows(self.cube, own), table):
            part, kept = expert_forward(pieces, column, *self.weights)
            results += halves(part)
            saved.append(kept)
        return reduce_rows(self.cube, *results), saved

    def backward(self, grad, table, saved):
        results, weights = [], []
        for pieces, column, kept in zip(gather_rows(self.cube, grad), table, saved):
            grad_in, weight_grads = expert_backward(pieces, column, kept, *self.weights)
            results += halves(grad_in)
            weights.append(weight_grads)
        return reduce_rows(self.cube, *results), jax.tree.map(jnp.add, *weights)


class Buckets:
    def __init__(self, cube, routes, gates, weights, capacity):
        self.cube, self.weights, self.capacity = cube, weights, capacity
        micros, self.rows, self.top = routes.shape
        self.experts = lax.axis_size("dp")
        self.tables = []
        for m in range(micros):
            flat = routes[m].reshape(-1)
            onehot = (flat[:, None] == jnp.arange(self.experts, dtype=jnp.int32)).astype(jnp.int32)
            earlier = jnp.cumsum(onehot, axis=0) - onehot
            target = flat * capacity + jnp.sum(earlier * onehot, axis=1)
            source = jnp.full((self.experts * capacity,), flat.shape[0], jnp.int32)
            source = source.at[target].set(jnp.arange(flat.shape[0], dtype=jnp.int32))
            self.tables.append((target, source, gates[m]))

    def exchange(self, rows):
        shape = (self.experts, self.capacity, rows.shape[1])
        moved = lax.all_to_all(rows.reshape(shape), "dp", split_axis=0, concat_axis=0, tiled=True)
        return moved.reshape(rows.shape)

    def whole(self, own):
        return jnp.concatenate([own, swap(own, self.cube.z)], axis=0)

    def folded(self, total):
        own, other = halves(total.astype(bf16))
        return wide(own) + wide(swap(other, self.cube.z))

    def forward(self, own, table):
        target, source, gates = table
        padded = jnp.pad(self.whole(own), ((0, 1), (0, 0)))
        arrived = self.exchange(jnp.take(padded, source // self.top, axis=0))
        part, saved = expert_forward([arrived], None, *self.weights)
        picked = jnp.take(self.exchange(part), target, axis=0).reshape(self.rows, self.top, -1)
        return self.folded(jnp.sum(gates[:, :, None] * picked, axis=1)), saved

    def backward(self, grad, table, saved):
        target, source, gates = table
        scaled = (gates[:, :, None] * wide(self.whole(grad))[:, None, :]).astype(bf16)
        padded = jnp.pad(scaled.reshape(self.rows * self.top, -1), ((0, 1), (0, 0)))
        arrived = self.exchange(jnp.take(padded, source, axis=0))
        grad_in, weights = expert_backward([arrived], None, saved, *self.weights)
        picked = jnp.take(self.exchange(grad_in), target, axis=0).reshape(self.rows, self.top, -1)
        return self.folded(jnp.sum(picked, axis=1, dtype=f32)), weights


def local(
    tokens, lengths, routes, gates, attn_gain, q_weight, key_projection, value_projection,
    o_weight, mlp_gain, expert_gate, expert_up, expert_down, cotangent,
):
    cube = Cube()
    section = lax.axis_index("section")
    shard = lax.axis_index("shard")
    me = lax.axis_index("dp")
    peers, shards = lax.axis_size("dp"), lax.axis_size("shard")
    micros, block_rows, model = tokens.shape
    rows = block_rows // shards
    first = section == 0

    starts, masks = [], []
    for m in range(micros):
        lens = lengths[m, 0]
        ends = jnp.cumsum(lens)
        longest = jnp.argmax(lens)
        start = ends[longest] - lens[longest]
        starts.append(start)
        position = (jnp.arange(rows, dtype=jnp.int32) + start + rows * shard) % block_rows
        segment = jnp.sum((position[:, None] >= ends[None, :]).astype(jnp.int32), axis=1)
        allowed = (segment[:, None] == segment[None, :]) & (position[None, :] <= position[:, None])
        masks.append(allowed.astype(f32))

    def turned(array, m, count=rows):
        doubled = jnp.concatenate([array, array], axis=0)
        return lax.dynamic_slice_in_dim(doubled, (starts[m] + rows * shard) % block_rows, count, 0)

    def pick(array, slot):
        here, there = array[min(slot, micros - 1)], array[max(slot - 1, 0)]
        return jax.tree.map(lambda a, b: jnp.where(first, a, b), here, there)

    zero_rows = jnp.zeros((rows, model), bf16)
    token_rows = [jnp.where(first, turned(tokens[m], m), zero_rows) for m in range(micros)]
    cot_rows = [jnp.where(first, zero_rows, turned(cotangent[m], m)) for m in range(micros)]

    qkv_own = jnp.concatenate([q_weight[0], key_projection[0], value_projection[0]], axis=1)
    out_own = o_weight[0]

    def other_half(weight):
        share = model // peers
        piece = lax.dynamic_slice_in_dim(weight, me * share, share, 0)
        return lax.all_gather(swap(piece, cube.z), "dp", axis=0, tiled=True)

    qkv_w = (qkv_own, other_half(qkv_own))
    out_w = (out_own, other_half(out_own))
    w_gate, w_up, w_down = expert_gate[0, 0], expert_up[0, 0], expert_down[0, 0]
    gain_one, gain_two = attn_gain[0][None], mlp_gain[0][None]

    routed = jnp.stack([turned(routes[0, m], m, block_rows) for m in range(micros)])
    weighed = jnp.stack([turned(gates[0, m], m, block_rows) for m in range(micros)])
    capacity = 2 * block_rows * routes.shape[3] // peers
    if capacity < block_rows:
        mixture = Buckets(cube, routed, weighed, (w_gate, w_up, w_down), capacity)
    else:
        mixture = Blocks(cube, routed, weighed, (w_gate, w_up, w_down))

    states, outs = [], []
    arriving = zero_rows
    for slot in range(micros + 1):
        fresh = token_rows[slot] if slot < micros else zero_rows
        inputs = wide(fresh + arriving)
        allowed = pick(masks, slot)
        hidden, normed_two, projected, heads = attention_forward(
            inputs, allowed, gain_one, gain_two, qkv_w, out_w
        )
        table = pick(mixture.tables, slot)
        total, saved = mixture.forward(normed_two, table)
        result = (hidden + total).astype(bf16)
        if slot < micros:
            arriving = lax.ppermute(result, "section", [(0, 1)])
        outs.append(result)
        states.append((inputs, hidden, allowed, projected, heads, table, saved))

    expert_sums = None
    coming = zero_rows
    attn_factors, gain_sums, input_grads = [], [], []
    for turn in range(micros + 1):
        inputs, hidden, allowed, projected, heads, table, saved = states[micros - turn]
        grad = coming + (cot_rows[micros - 1 - turn] if turn < micros else zero_rows)
        grad_two, weight_grads = mixture.backward(grad, table, saved)
        expert_sums = (
            weight_grads if expert_sums is None else jax.tree.map(jnp.add, expert_sums, weight_grads)
        )
        grad_input, grad_low, normed, grads, attn_g, mlp_g = attention_backward(
            wide(grad), grad_two, inputs, hidden, allowed, gain_one, gain_two, projected, qkv_w, out_w
        )
        if turn < micros:
            coming = lax.ppermute(grad_input.astype(bf16), "section", [(1, 0)])
        attn_factors.append((normed, grad_low, grads, heads))
        gain_sums.append(jnp.concatenate([attn_g, mlp_g], axis=0))
        input_grads.append(grad_input)

    normed_t = jnp.concatenate([f[0] for f in attn_factors], axis=0).T
    grad_t = jnp.concatenate([f[1] for f in attn_factors], axis=0).T
    full = []
    for g in range(shards):
        grad_qkv = jnp.concatenate([f[2][g] for f in attn_factors], axis=0)
        head_rows = jnp.concatenate([f[3][g] for f in attn_factors], axis=0)
        both = jnp.concatenate([dot_nn(normed_t, grad_qkv), dot_nn(grad_t, head_rows)], axis=1)
        full.append(both.astype(bf16).reshape(peers, model // peers, -1))

    def weight_group(group):
        blocks = []
        for m, s in group:
            block = jnp.take(full[s], me ^ (m ^ cube.inner), axis=0)
            blocks.append(block.reshape(-1, block.shape[2]))
        return jnp.concatenate(blocks, axis=0)

    total = reduce_rows(
        cube,
        weight_group(cube.near),
        weight_group(cube.mate(cube.near)),
        weight_group(cube.far),
        weight_group(cube.mate(cube.far)),
    )
    width = q_weight.shape[2]
    grad_q = total[:, :width]
    grad_k = total[:, width : width + HEAD_SIZE]
    grad_v = total[:, width + HEAD_SIZE : width + 2 * HEAD_SIZE]
    grad_o = total[:, width + 2 * HEAD_SIZE :]
    gain_total = lax.psum(sum(gain_sums), ("dp", "shard"))
    share = model // peers
    gain_total = lax.dynamic_slice_in_dim(gain_total, me * share, share, 1)

    def placed(own, m):
        half = model // shards
        kept = lax.dynamic_slice_in_dim(own, shard * half, half, 1)
        given = lax.dynamic_slice_in_dim(own, (1 - shard) * half, half, 1)
        got = swap(given, cube.z)
        low = jnp.where(shard == 0, kept, got)
        high = jnp.where(shard == 0, got, kept)
        return lax.dynamic_slice_in_dim(
            jnp.concatenate([low, high, low, high], axis=0), (block_rows - starts[m]) % block_rows, block_rows, 0
        )

    section_out = jnp.stack(
        [placed(jnp.where(first, outs[m], outs[m + 1]), m) for m in range(micros)]
    )
    input_grad = jnp.stack(
        [
            placed(jnp.where(first, input_grads[micros - m], input_grads[micros - m - 1]), m)
            for m in range(micros)
        ]
    )
    gate_total, up_total, down_total = expert_sums
    return (
        section_out[None],
        input_grad[None],
        gain_total[0][None],
        grad_q[None],
        grad_k[None],
        grad_v[None],
        grad_o[None],
        gain_total[1][None],
        gate_total[None, None],
        up_total[None, None],
        down_total[None, None],
    )


def solution(mesh):
    in_specs = (
        P(None, "dp", None),
        P(None, "dp", None),
        P("section", None, "dp", None),
        P("section", None, "dp", None),
        P("section", None),
        P("section", None, "shard"),
        P("section", None, "shard"),
        P("section", None, "shard"),
        P("section", None, "shard"),
        P("section", None),
        P("section", "dp", None, "shard"),
        P("section", "dp", None, "shard"),
        P("section", "dp", "shard", None),
        P(None, "dp", None),
    )
    out_specs = (
        P("section", None, "dp", "shard"),
        P("section", None, "dp", "shard"),
        P("section", "dp"),
        P("section", "dp", "shard"),
        P("section", "dp", "shard"),
        P("section", "dp", "shard"),
        P("section", "dp", "shard"),
        P("section", "dp"),
        P("section", "dp", None, "shard"),
        P("section", "dp", None, "shard"),
        P("section", "dp", "shard", None),
    )
    return jax.shard_map(local, mesh=mesh, in_specs=in_specs, out_specs=out_specs, check_vma=False)
```

time: 2160 us -> 902 us (0.42)
  waiting for transfers between devices: 984 us -> 292 us
  blocking collectives: 393 us -> 95.4 us
  local copies, waits for them, and re-layouts: 281 us -> 71.6 us
  other arithmetic: 191 us -> 64.9 us
  starting transfers between devices: 48.5 us -> 148 us
  matrix products: 237 us -> 198 us
    psum x11 -> x0, waiting for transfers between devices: 447 us -> none  [the longest x3 169 us: layer_forward(): attention = lax.psum(contract_cols(head_out, w_out), 'shard')]
    all_to_all x5 -> x0, blocking collectives: 379 us -> none  [the longest x2 151 us: layer_backward(): lax.all_to_all(outgoing, 'dp', split_axis=0, concat_axis=0, tiled=True)]
    all_to_all x7 -> x0, waiting for transfers between devices: 373 us -> none  [the longest x3 203 us: layer_forward(): lax.all_to_all(partial_rows, 'dp', split_axis=0, concat_axis=0, tiled=True)]
    ppermute x4 -> x165, waiting for transfers between devices: 96.4 us -> 252 us  [the longest x161 215 us: swap(): lax.ppermute(value, axis, [(i, i ^ bit) for i in range(lax.axis_size(axis...]
    gather x12 -> x2, local copies, waits for them, and re-layouts: 142 us -> 1.4 us  [ordered(): weighed = jnp.take(column, jnp.concatenate(order), axis=0)]
    ppermute x4 -> x165, starting transfers between devices: 11.9 us -> 148 us  [the longest x161 135 us: swap(): lax.ppermute(value, axis, [(i, i ^ bit) for i in range(lax.axis_size(axis...]
    reduce_scatter x4 -> x0, waiting for transfers between devices: 67.9 us -> none  [the longest x1 43.9 us: local(): lax.psum_scatter(query_sum.astype(jnp.bfloat16), 'dp', scatter_dimension=...]
    psum x0 -> x1, blocking collectives: none -> 66.9 us  [local(): gain_total = lax.psum(sum(gain_sums), ('dp', 'shard'))]
  transfers between devices with their start and end apart: 26 -> 167, of which waited for: 25 -> 94; matrix products, arithmetic and copies ran while one was open for 11% -> 29% of each run, Pallas kernels for 0% -> 0%
where the time goes in v1:
time: 902 us; the launch traced here: 896 us
  waiting for transfers between devices  292 us (32%)
  matrix products  198 us (22%)
  starting transfers between devices  148 us (16%)
  blocking collectives  95.4 us (11%)
  local copies, waits for them, and re-layouts  71.6 us (8%)
  other arithmetic  64.9 us (7%)
  between operations  26.2 us (3%)
    ppermute x161, waiting for transfers between devices, swap(): lax.ppermute(value, axis, [(i, i ^ bit) for i in range(lax.axis_size(axis...  215 us
    ppermute x161, starting transfers between devices, swap(): lax.ppermute(value, axis, [(i, i ^ bit) for i in range(lax.axis_size(axis...  135 us
    dot_general x30, matrix products, dot_tn(): lax.dot_general(a, b, (((0,), (0,)), ((), ())), preferred_element_type=f32)  70.2 us
    psum x1, blocking collectives, local(): gain_total = lax.psum(sum(gain_sums), ('dp', 'shard'))  66.9 us
    dot_general x42, matrix products, dot_nt(): lax.dot_general(a, b, (((1,), (1,)), ((), ())), preferred_element_type=f32)  64.8 us
    dot_general x46, matrix products, dot_nn(): lax.dot_general(a, b, (((1,), (0,)), ((), ())), preferred_element_type=f32)  63 us
    unnamed x625, local copies, waits for them, and re-layouts  44.2 us
    all_gather x2, waiting for transfers between devices, other_half(): return lax.all_gather(swap(piece, cube.z), 'dp', axis=0, tiled=True)  40 us
  transfers between devices with their start and end apart: 167, of which 94 were waited for; matrix products, arithmetic and copies ran while one was open for 29% of the time, Pallas kernels for 0%

profile of v1, /device:TPU:0, one launch (start us, length us, event | category | flops | bytes accessed | tf_op | source)
XLA Modules:
  0.0 896.3 jit_solution(9406850469543230741)
XLA Ops:
  34.9 28.5 %all-gather = f32[32,128,8]{1,2,0:T(8,128)S(1)} all-gather(f32[2,128,8]{1,2,0:T(8,128)S(1)} %select_reduce_fusion), channel_id=2, replica_groups=mesh['section'=2,'dp'=8,'shard'=2] {'dp','shard'}, dimensions={0}, use_global_device_ids=true | all-gather | bytes 139264 | tf_op jit(solution)/shard_map/all_gather | solution.py:232
  88.8 16.7 %all-gather.4.cloned.1.call-done = bf16[1536,1024]{1,0:T(8,128)(2,1)} async-done(((bf16[192,1024]{1,0:T(8,128)(2,1)}), bf16[1536,1024]{1,0:T(8,128)(2,1)}) %all-gather.4.cloned.1.call-update) | async-done | bytes 3145744 | tf_op jit(solution)/shard_map/all_gather | solution.py:349
  113.1 23.3 %all-gather.6.cloned.1.call-done = bf16[1536,768]{1,0:T(8,128)(2,1)} async-done(((bf16[192,768]{1,0:T(8,128)(2,1)}), bf16[1536,768]{1,0:T(8,128)(2,1)}) %all-gather.6.cloned.1.call-update) | async-done | bytes 2359312 | tf_op jit(solution)/shard_map/all_gather | solution.py:349
  144.3 6.5 collective-permute-done.4
  154.5 6.9 collective-permute-done.10
  197.5 6.7 collective-permute-done.79
  221.9 8.2 collective-permute-done.19
  255.3 7.6 collective-permute-start.29
  275.9 6.1 collective-permute-done.35
  321.5 5.8 collective-permute-done.43
  332.3 6.9 collective-permute-done.44
  350.1 6.3 collective-permute-done.52
  361.8 7.3 collective-permute-start.55
  384.0 8.8 collective-permute-done.61
  507.4 9.8 %collective-permute-done.102 = bf16[128,1536]{1,0:T(8,128)(2,1)S(1)} collective-permute-done((bf16[128,1536]{1,0:T(8,128)(2,1)S(1)}, bf16[128,1536]{1,0:T(8,128)(2,1)S(1)}, u32[]{:S(2)}, u32[]{:S(2)}) %collective-permute-start.102) | collective-permute-done | bytes 393248 | tf_op jit(solution)/shard_map/ppermute | solution.py:395
  530.8 7.9 collective-permute-done.111
  582.4 5.8 collective-permute-done.119
  616.4 15.3 %collective-permute-done.127 = bf16[128,1536]{1,0:T(8,128)(2,1)S(1)} collective-permute-done((bf16[128,1536]{1,0:T(8,128)(2,1)S(1)}, bf16[128,1536]{1,0:T(8,128)(2,1)S(1)}, u32[]{:S(2)}, u32[]{:S(2)}) %collective-permute-start.127) | collective-permute-done | bytes 393248 | tf_op jit(solution)/shard_map/ppermute | solution.py:395
  647.6 7.4 collective-permute-done.136
  699.0 5.8 convolution_add_fusion
  717.6 5.9 collective-permute-done.144
  762.7 6.8 fusion.8
  792.9 66.9 %psum.7 = f32[2,1536]{1,0:T(2,128)} all-reduce(f32[2,1536]{1,0:T(2,128)S(1)} %fusion.336), channel_id=1, replica_groups=mesh['section'=2,'dp'=8,'shard'=2] {'dp','shard'}, use_global_device_ids=true, to_apply=%region_43.45 | all-reduce | flops 3072 | bytes 24576 | tf_op jit(solution)/shard_map/psum | solution.py:428
  875.3 6.0 collective-permute-done.158
  (1302 shorter events, 586.9 us)
Async XLA Ops:
  7.2 98.3 %all-gather.4.cloned.1.call-start = ((), (), s32[]{:S(2)}) async-start(), calls=%async_computation | async-start | bytes 3538944 | tf_op jit(solution)/shard_map/all_gather | solution.py:349
  9.6 76.4 %collective-permute-start.1 = (bf16[192,768]{1,0:T(8,128)(2,1)}, bf16[192,768]{1,0:T(8,128)(2,1)}, u32[]{:S(2)}, u32[]{:S(2)}) collective-permute-start(bf16[192,768]{1,0:T(8,128)(2,1)} %dynamic-slice_bitcast_fusion), channel_id=1, source_target_pairs={{0,1},{1,0},{2,3},{3,2},{4,5},{5,4},{6,7},{7,6},{8,9},{9,8},{10,11... | collective-permute-start | bytes 884744 | tf_op jit(solution)/shard_map/ppermute | solution.py:54
  17.5 56.2 %collective-permute-start = (bf16[192,1024]{1,0:T(8,128)(2,1)}, bf16[192,1024]{1,0:T(8,128)(2,1)}, u32[]{:S(2)}, u32[]{:S(2)}) collective-permute-start(bf16[192,1024]{1,0:T(8,128)(2,1)} %constant_dynamic-slice_fusion.15), channel_id=1, source_target_pairs={{0,1},{1,0},{2,3},{3,2},{4,5},{5,4},{6,7},{7,6},{8,9},{9,8},{10,11... | collective-permute-start | bytes 1179656 | tf_op jit(solution)/shard_map/ppermute | solution.py:54
  29.1 179.8 %collective-permute-start.80 = (bf16[128,1536]{1,0:T(8,128)(2,1)}, bf16[128,1536]{1,0:T(8,128)(2,1)}, u32[]{:S(2)}, u32[]{:S(2)}) collective-permute-start(bf16[128,1536]{1,0:T(8,128)(2,1)} %get-tuple-element.50), channel_id=1, source_target_pairs={{0,1},{1,0},{2,3},{3,2},{4,5},{5,4},{6,7},{7,6},{8,9},{9,8},{10,11... | collective-permute-start | bytes 1179656 | tf_op jit(solution)/shard_map/ppermute | solution.py:54
  73.7 62.7 %all-gather.6.cloned.1.call-start = ((), (), s32[]{:S(2)}) async-start(), calls=%async_computation.1 | async-start | bytes 2654208 | tf_op jit(solution)/shard_map/all_gather | solution.py:349
  185.0 23.9 %collective-permute-start.7 = (bf16[512,1536]{1,0:T(8,128)(2,1)}, bf16[512,1536]{1,0:T(8,128)(2,1)}, u32[]{:S(2)}, u32[]{:S(2)}) collective-permute-start(bf16[512,1536]{1,0:T(8,128)(2,1)} %slice.1429), channel_id=1, source_target_pairs={{0,2},{2,0},{4,6},{6,4},{8,10},{10,8},{12,14},{14,12},{1,3},{3,1},... | collective-permute-start | bytes 4718600 | tf_op jit(solution)/shard_map/ppermute | solution.py:54
  208.9 29.3 %collective-permute-start.81 = (bf16[128,1536]{1,0:T(8,128)(2,1)}, bf16[128,1536]{1,0:T(8,128)(2,1)S(1)}, u32[]{:S(2)}, u32[]{:S(2)}) collective-permute-start(bf16[128,1536]{1,0:T(8,128)(2,1)} %get-tuple-element.50), channel_id=1, source_target_pairs={{0,2},{2,0},{4,6},{6,4},{8,10},{10,8},{12,14},{14,12},{1,3},{3,1},... | collective-permute-start | bytes 1179656 | tf_op jit(solution)/shard_map/ppermute | solution.py:54
  208.9 55.7 %collective-permute-start.86 = (bf16[128,1536]{1,0:T(8,128)(2,1)}, bf16[128,1536]{1,0:T(8,128)(2,1)S(1)}, u32[]{:S(2)}, u32[]{:S(2)}) collective-permute-start(bf16[128,1536]{1,0:T(8,128)(2,1)} %collective-permute-done.80), channel_id=1, source_target_pairs={{0,4},{2,6},{4,0},{6,2},{8,12},{10,14},{12,8},{14,10},{1,5},{3,7},... | collective-permute-start | bytes 1179656 | tf_op jit(solution)/shard_map/ppermute | solution.py:54
  240.3 79.6 %collective-permute-start.88 = (bf16[48,1536]{1,0:T(8,128)(2,1)S(1)}, bf16[48,1536]{1,0:T(8,128)(2,1)S(1)}, u32[]{:S(2)}, u32[]{:S(2)}) collective-permute-start(bf16[48,1536]{1,0:T(8,128)(2,1)S(1)} %slice.1553), channel_id=1, source_target_pairs={{0,4},{2,6},{4,0},{6,2},{8,12},{10,14},{12,8},{14,10},{1,5},{3,7},... | collective-permute-start | bytes 442376 | tf_op jit(solution)/shard_map/ppermute | solution.py:54
  320.0 27.4 %collective-permute-start.82 = (bf16[384,1536]{1,0:T(8,128)(2,1)S(1)}, bf16[384,1536]{1,0:T(8,128)(2,1)S(1)}, u32[]{:S(2)}, u32[]{:S(2)}) collective-permute-start(bf16[384,1536]{1,0:T(8,128)(2,1)S(1)} %pad_maximum_fusion.9), channel_id=1, source_target_pairs={{0,2},{2,0},{4,6},{6,4},{8,10},{10,8},{12,14},{14,12},{1,3},{3,1},... | collective-permute-start | bytes 3538952 | tf_op jit(solution)/shard_map/ppermute | solution.py:54
  339.3 31.8 %collective-permute-start.91 = (bf16[128,1536]{1,0:T(8,128)(2,1)S(1)}, bf16[128,1536]{1,0:T(8,128)(2,1)S(1)}, u32[]{:S(2)}, u32[]{:S(2)}) collective-permute-start(bf16[128,1536]{1,0:T(8,128)(2,1)S(1)} %pad_maximum_fusion.24), channel_id=1, source_target_pairs={{0,2},{2,0},{4,6},{6,4},{8,10},{10,8},{12,14},{14,12},{1,3},{3,1},... | collective-permute-start | bytes 1179656 | tf_op jit(solution)/shard_map/ppermute | solution.py:54
  349.5 22.5 %collective-permute-start.51 = (bf16[128,768]{1,0:T(8,128)(2,1)S(1)}, bf16[128,768]{1,0:T(8,128)(2,1)S(1)}, u32[]{:S(2)}, u32[]{:S(2)}) collective-permute-start(bf16[128,768]{1,0:T(8,128)(2,1)S(1)} %constant_dynamic-slice_fusion.6), channel_id=1, source_target_pairs={{0,1},{1,0},{2,3},{3,2},{4,5},{5,4},{6,7},{7,6},{8,9},{9,8},{10,11... | collective-permute-start | bytes 589832 | tf_op jit(solution)/shard_map/ppermute | solution.py:54
  395.6 20.6 %collective-permute-start.65 = (bf16[384,1536]{1,0:T(8,128)(2,1)S(1)}, bf16[384,1536]{1,0:T(8,128)(2,1)S(1)}, u32[]{:S(2)}, u32[]{:S(2)}) collective-permute-start(bf16[384,1536]{1,0:T(8,128)(2,1)S(1)} %pad_maximum_fusion.8), channel_id=1, source_target_pairs={{0,2},{2,0},{4,6},{6,4},{8,10},{10,8},{12,14},{14,12},{1,3},{3,1},... | collective-permute-start | bytes 3538952 | tf_op jit(solution)/shard_map/ppermute | solution.py:54
  410.7 62.2 %collective-permute-start.58 = (bf16[512,1536]{1,0:T(8,128)(2,1)S(1)}, bf16[512,1536]{1,0:T(8,128)(2,1)}, u32[]{:S(2)}, u32[]{:S(2)}) collective-permute-start(bf16[512,1536]{1,0:T(8,128)(2,1)S(1)} %slice.1528), channel_id=1, source_target_pairs={{0,2},{2,0},{4,6},{6,4},{8,10},{10,8},{12,14},{14,12},{1,3},{3,1},... | collective-permute-start | bytes 4718600 | tf_op jit(solution)/shard_map/ppermute | solution.py:54
  416.2 43.5 %collective-permute-start.83 = (bf16[512,1536]{1,0:T(8,128)(2,1)}, bf16[512,1536]{1,0:T(8,128)(2,1)}, u32[]{:S(2)}, u32[]{:S(2)}) collective-permute-start(bf16[512,1536]{1,0:T(8,128)(2,1)} %slice.1548), channel_id=1, source_target_pairs={{0,2},{2,0},{4,6},{6,4},{8,10},{10,8},{12,14},{14,12},{1,3},{3,1},... | collective-permute-start | bytes 4718600 | tf_op jit(solution)/shard_map/ppermute | solution.py:54
  482.9 20.7 %collective-permute-start.70 = (bf16[128,1536]{1,0:T(8,128)(2,1)S(1)}, bf16[128,1536]{1,0:T(8,128)(2,1)S(1)}, u32[]{:S(2)}, u32[]{:S(2)}) collective-permute-start(bf16[128,1536]{1,0:T(8,128)(2,1)S(1)} %get-tuple-element.85), channel_id=1, source_target_pairs={{0,4},{2,6},{4,0},{6,2},{8,12},{10,14},{12,8},{14,10},{1,5},{3,7},... | collective-permute-start | bytes 1179656 | tf_op jit(solution)/shard_map/ppermute | solution.py:54
  561.5 20.9 %collective-permute-start.108 = (bf16[512,1536]{1,0:T(8,128)(2,1)S(1)}, bf16[512,1536]{1,0:T(8,128)(2,1)S(1)}, u32[]{:S(2)}, u32[]{:S(2)}) collective-permute-start(bf16[512,1536]{1,0:T(8,128)(2,1)S(1)} %slice.1592), channel_id=1, source_target_pairs={{0,2},{2,0},{4,6},{6,4},{8,10},{10,8},{12,14},{14,12},{1,3},{3,1},... | collective-permute-start | bytes 4718600 | tf_op jit(solution)/shard_map/ppermute | solution.py:54
  643.4 22.1 %collective-permute-start.132 = (bf16[384,1536]{1,0:T(8,128)(2,1)S(1)}, bf16[384,1536]{1,0:T(8,128)(2,1)S(1)}, u32[]{:S(2)}, u32[]{:S(2)}) collective-permute-start(bf16[384,1536]{1,0:T(8,128)(2,1)S(1)} %pad_maximum_fusion.13), channel_id=1, source_target_pairs={{0,2},{2,0},{4,6},{6,4},{8,10},{10,8},{12,14},{14,12},{1,3},{3,1},... | collective-permute-start | bytes 3538952 | tf_op jit(solution)/shard_map/ppermute | solution.py:54
  672.9 44.7 %collective-permute-start.133 = (bf16[512,1536]{1,0:T(8,128)(2,1)}, bf16[512,1536]{1,0:T(8,128)(2,1)}, u32[]{:S(2)}, u32[]{:S(2)}) collective-permute-start(bf16[512,1536]{1,0:T(8,128)(2,1)} %slice.1636), channel_id=1, source_target_pairs={{0,2},{2,0},{4,6},{6,4},{8,10},{10,8},{12,14},{14,12},{1,3},{3,1},... | collective-permute-start | bytes 4718600 | tf_op jit(solution)/shard_map/ppermute | solution.py:54
  772.3 88.9 %collective-permute-start.154 = (bf16[768,1792]{1,0:T(8,128)(2,1)}, bf16[768,1792]{1,0:T(8,128)(2,1)}, u32[]{:S(2)}, u32[]{:S(2)}) collective-permute-start(bf16[768,1792]{1,0:T(8,128)(2,1)} %pad_maximum_fusion.1), channel_id=1, source_target_pairs={{0,2},{2,0},{4,6},{6,4},{8,10},{10,8},{12,14},{14,12},{1,3},{3,1},... | collective-permute-start | bytes 8257544 | tf_op jit(solution)/shard_map/ppermute | solution.py:54
  786.8 74.5 %collective-permute-start.157 = (bf16[192,1792]{1,0:T(8,128)(2,1)}, bf16[192,1792]{1,0:T(8,128)(2,1)}, u32[]{:S(2)}, u32[]{:S(2)}) collective-permute-start(bf16[192,1792]{1,0:T(8,128)(2,1)} %get-tuple-element.107), channel_id=1, source_target_pairs={{0,8},{2,10},{4,12},{6,14},{8,0},{10,2},{12,4},{14,6},{1,9},{3,11}... | collective-permute-start | bytes 2064392 | tf_op jit(solution)/shard_map/ppermute | solution.py:54
  787.3 74.1 %collective-permute-start.163 = (bf16[192,1792]{1,0:T(8,128)(2,1)}, bf16[192,1792]{1,0:T(8,128)(2,1)}, u32[]{:S(2)}, u32[]{:S(2)}) collective-permute-start(bf16[192,1792]{1,0:T(8,128)(2,1)} %get-tuple-element.108), channel_id=1, source_target_pairs={{0,4},{2,6},{4,0},{6,2},{8,12},{10,14},{12,8},{14,10},{1,5},{3,7},... | collective-permute-start | bytes 2064392 | tf_op jit(solution)/shard_map/ppermute | solution.py:54
  788.5 72.8 %collective-permute-start.160 = (bf16[192,1792]{1,0:T(8,128)(2,1)}, bf16[192,1792]{1,0:T(8,128)(2,1)}, u32[]{:S(2)}, u32[]{:S(2)}) collective-permute-start(bf16[192,1792]{1,0:T(8,128)(2,1)} %get-tuple-element.109), channel_id=1, source_target_pairs={{0,1},{1,0},{2,3},{3,2},{4,5},{5,4},{6,7},{7,6},{8,9},{9,8},{10,11... | collective-permute-start | bytes 2064392 | tf_op jit(solution)/shard_map/ppermute | solution.py:54
  791.6 77.3 %collective-permute-start.153 = (f32[128,768]{1,0:T(8,128)}, f32[128,768]{1,0:T(8,128)S(1)}, u32[]{:S(2)}, u32[]{:S(2)}) collective-permute-start(f32[128,768]{1,0:T(8,128)} %constant_dynamic-slice_fusion.3), channel_id=1, source_target_pairs={{0,1},{1,0},{2,3},{3,2},{4,5},{5,4},{6,7},{7,6},{8,9},{9,8},{10,11... | collective-permute-start | bytes 1179656 | tf_op jit(solution)/shard_map/ppermute | solution.py:54
  (359 other events, 2764.3 us)
Sparse Core Ops, SparseCore 0:
  73.8 31.5 all-gather.3
  107.3 29.0 all-gather.5

commit v2 on v1

--- a/solution.py
+++ b/solution.py
@@ -42,11 +42,12 @@
             inner = inner + [m | bit for m in inner]
         self.inner = np.array(inner)
         x, y = self.x[1], self.y[1]
-        self.near = [(0, 0), (x, 0), (y, 0), (0, 1)]
-        self.far = [(x | y, 0), (y, 1), (x, 1), (x | y, 1)]
-
-    def mate(self, group):
-        return [(m | self.core[1], s) for m, s in group]
+        near = [(0, 0), (x, 0), (y, 0), (0, 1)]
+        middle = [(x | y, 0), (y, 1), (x, 1)]
+        last = [(x | y, 1)]
+        self.stages = [
+            (group, [(m | self.core[1], s) for m, s in group]) for group in (near, middle, last)
+        ]
 
 
 def swap(value, direction):
@@ -59,52 +60,49 @@
     return [(0, step), (step, 2 * step), (2 * step, rows)]
 
 
-def gather_rows(cube, own):
+def gather_rows(cube, own, work):
     for direction in cube.extra:
         own = jnp.concatenate([own, swap(own, direction)], axis=0)
-    rx, ry, rz = swap(own, cube.x), swap(own, cube.y), swap(own, cube.z)
+    near = [swap(own, d) for d in (cube.x, cube.y, cube.z)]
     own_mate = swap(own, cube.core)
-    rxy, ryz, rzx = swap(rx, cube.y), swap(ry, cube.z), swap(rz, cube.x)
-    near_mate = swap(jnp.concatenate([rx, ry, rz], axis=0), cube.core)
+    middle = [swap(block, d) for block, d in zip(near, (cube.y, cube.z, cube.x))]
+    near_mate = swap(jnp.concatenate(near, axis=0), cube.core)
+    done = [work(0, [own, *near, own_mate, near_mate])]
+    middle, done = lax.optimization_barrier((middle, done))
     cuts = thirds(own.shape[0])
     last = [
-        swap(block[lo:hi], direction)
-        for block, direction, (lo, hi) in zip((rxy, ryz, rzx), (cube.z, cube.x, cube.y), cuts)
+        swap(block[lo:hi], d) for block, d, (lo, hi) in zip(middle, (cube.z, cube.x, cube.y), cuts)
     ]
-    far_mate = swap(jnp.concatenate([rxy, ryz, rzx], axis=0), cube.core)
-    rxyz = jnp.concatenate(last, axis=0)
-    last_mate = swap(rxyz, cube.core)
-    near = [own, rx, ry, rz, own_mate, near_mate]
-    far = [rxy, ryz, rzx, rxyz, far_mate, last_mate]
-    return near, far
+    middle_mate = swap(jnp.concatenate(middle, axis=0), cube.core)
+    done.append(work(1, [*middle, middle_mate]))
+    last = jnp.concatenate(last, axis=0)
+    done.append(work(2, [last, swap(last, cube.core)]))
+    return done
 
 
 def low_sum(*terms):
     return sum(wide(t) for t in terms).astype(bf16)
 
 
-def reduce_rows(cube, near, near_mate, far, far_mate):
-    rows = near.shape[0] // 4
-    far_in = swap(far_mate, cube.core)
-    near_in = swap(near_mate, cube.core)
-    far_sum = low_sum(far, far_in)
+def reduce_rows(cube, stages):
+    (near, near_mate), (middle, middle_mate), (last, last_mate) = stages
+    rows = last.shape[0]
+    last_in, middle_in, near_in = [swap(t, cube.core) for t in (last_mate, middle_mate, near_mate)]
+
+    def block(i, *groups):
+        return [g[i * rows : (i + 1) * rows] for g in groups]
+
     cuts = thirds(rows)
-    sent = far_sum[3 * rows :]
-    directions = (cube.z, cube.x, cube.y)
-    arrived = [swap(sent[lo:hi], d) for d, (lo, hi) in zip(directions, cuts)]
-    middle = []
-    for i, (lo, hi) in enumerate(cuts):
-        block = far_sum[i * rows : (i + 1) * rows]
-        middle.append(
-            low_sum(block, jnp.pad(arrived[i], ((lo, rows - hi), (0, 0))))
-        )
-    back = [swap(middle[0], cube.y), swap(middle[1], cube.z), swap(middle[2], cube.x)]
-    outer = [
-        low_sum(near[i * rows : (i + 1) * rows], near_in[i * rows : (i + 1) * rows], back[i - 1])
-        for i in (1, 2, 3)
+    sent = low_sum(last, last_in)
+    arrived = [swap(sent[lo:hi], d) for d, (lo, hi) in zip((cube.z, cube.x, cube.y), cuts)]
+    sent = [
+        low_sum(*block(i, middle, middle_in), jnp.pad(arrived[i], ((lo, rows - hi), (0, 0))))
+        for i, (lo, hi) in enumerate(cuts)
     ]
-    ends = [swap(t, d) for t, d in zip(outer, (cube.x, cube.y, cube.z))]
-    total = wide(near[:rows]) + wide(near_in[:rows]) + wide(ends[0]) + wide(ends[1]) + wide(ends[2])
+    arrived = [swap(t, d) for t, d in zip(sent, (cube.y, cube.z, cube.x))]
+    sent = [low_sum(*block(i + 1, near, near_in), arrived[i]) for i in range(3)]
+    arrived = [swap(t, d) for t, d in zip(sent, (cube.x, cube.y, cube.z))]
+    total = sum(wide(t) for t in block(0, near, near_in) + arrived)
     for direction in reversed(cube.extra):
         half = total.shape[0] // 2
         total = total[:half] + wide(swap(total[half:].astype(bf16), direction))
@@ -140,24 +138,19 @@
     return exp_scores / jnp.sum(exp_scores, axis=1, keepdims=True)
 
 
-def attention_forward(inputs, allowed, attn_gain, mlp_gain, qkv_w, out_w):
-    rows = inputs.shape[0]
-    normed = (inputs * norm_factor(inputs) * attn_gain).astype(bf16)
-    hidden = inputs
-    projected, heads = [], []
-    for w, w_out in zip(qkv_w, out_w):
-        qkv = dot_nn(normed, w).astype(bf16)
-        width = qkv.shape[1] - 2 * HEAD_SIZE
-        query = stack_heads(qkv[:, :width])
-        key, value = qkv[:, width : width + HEAD_SIZE], qkv[:, width + HEAD_SIZE :]
-        tiled = jnp.concatenate([allowed] * (width // HEAD_SIZE), axis=0)
-        probs = head_probs(query, key, tiled).astype(bf16)
-        head_out = spread_heads(dot_nn(probs, value).astype(bf16), rows)
-        hidden = hidden + dot_nt(head_out, w_out)
-        projected.append(qkv)
-        heads.append(head_out)
-    normed_two = (hidden * norm_factor(hidden) * mlp_gain).astype(bf16)
-    return hidden, normed_two, projected, heads
+def normed_rows(values, gain):
+    return (values * norm_factor(values) * gain).astype(bf16)
+
+
+def head_group(normed, allowed, w, w_out):
+    qkv = dot_nn(normed, w).astype(bf16)
+    width = qkv.shape[1] - 2 * HEAD_SIZE
+    query = stack_heads(qkv[:, :width])
+    key, value = qkv[:, width : width + HEAD_SIZE], qkv[:, width + HEAD_SIZE :]
+    tiled = jnp.concatenate([allowed] * (width // HEAD_SIZE), axis=0)
+    probs = head_probs(query, key, tiled).astype(bf16)
+    head_out = spread_heads(dot_nn(probs, value).astype(bf16), normed.shape[0])
+    return dot_nt(head_out, w_out), qkv, head_out
 
 
 def attention_backward(grad, grad_two, inputs, hidden, allowed, attn_gain, mlp_gain, projected, qkv_w, out_w):
@@ -223,39 +216,52 @@
 class Blocks:
     def __init__(self, cube, routes, gates, weights):
         self.cube, self.weights = cube, weights
-        me, shard = lax.axis_index("dp"), lax.axis_index("shard")
+        micros = routes.shape[0]
+        peers = lax.axis_size("dp")
         rows = routes.shape[1] // lax.axis_size("shard")
-        numbers = jnp.arange(lax.axis_size("dp"), dtype=jnp.int32)
-        table = jnp.sum(
-            jnp.where(routes[:, :rows, :, None] == numbers, gates[:, :rows, :, None], 0.0), axis=2
+        numbers = jnp.arange(peers, dtype=jnp.int32)[:, None, None]
+        table = jnp.concatenate(
+            [
+                jnp.sum(jnp.where(routes[m, :rows].T == numbers, gates[m, :rows].T, 0.0), axis=1)
+                for m in range(micros)
+            ],
+            axis=0,
         )
-        everyone = lax.all_gather(table, ("dp", "shard"), axis=0)
-        column = lax.dynamic_index_in_dim(everyone, me, 3, keepdims=False)
-
-        def ordered(group):
-            order = [(me ^ (m ^ cube.inner)) * lax.axis_size("shard") + (shard ^ s) for m, s in group]
-            weighed = jnp.take(column, jnp.concatenate(order), axis=0)
-            return [weighed[:, m].reshape(-1, 1) for m in range(routes.shape[0])]
-
-        near = ordered(cube.near + cube.mate(cube.near))
-        far = ordered(cube.far + cube.mate(cube.far))
-        self.tables = list(zip(near, far))
+        places = [(0, 0)]
+        for axis, bit in [*cube.extra, cube.core, cube.x, cube.y, cube.z]:
+            table = jnp.concatenate([table, swap(table, (axis, bit))], axis=1)
+            places += [(m | bit, s) if axis == "dp" else (m, s | bit) for m, s in places]
+        mine = [
+            lax.dynamic_index_in_dim(table, m * peers + lax.axis_index("dp"), 0, keepdims=False)
+            for m in range(micros)
+        ]
+
+        def ordered(values, groups):
+            order = [places.index((m ^ int(i), s)) for group in groups for m, s in group for i in cube.inner]
+            return jnp.concatenate([values[p * rows : (p + 1) * rows] for p in order]).reshape(-1, 1)
+
+        self.tables = [[ordered(values, groups) for groups in cube.stages] for values in mine]
 
     def forward(self, own, table):
-        results, saved = [], []
-        for pieces, column in zip(gather_rows(self.cube, own), table):
-            part, kept = expert_forward(pieces, column, *self.weights)
-            results += halves(part)
+        saved = []
+
+        def work(stage, pieces):
+            part, kept = expert_forward(pieces, table[stage], *self.weights)
             saved.append(kept)
-        return reduce_rows(self.cube, *results), saved
+            return halves(part)
+
+        return reduce_rows(self.cube, gather_rows(self.cube, own, work)), saved
 
     def backward(self, grad, table, saved):
-        results, weights = [], []
-        for pieces, column, kept in zip(gather_rows(self.cube, grad), table, saved):
-            grad_in, weight_grads = expert_backward(pieces, column, kept, *self.weights)
-            results += halves(grad_in)
+        weights = []
+
+        def work(stage, pieces):
+            grad_in, weight_grads = expert_backward(pieces, table[stage], saved[stage], *self.weights)
             weights.append(weight_grads)
-        return reduce_rows(self.cube, *results), jax.tree.map(jnp.add, *weights)
+            return halves(grad_in)
+
+        total = reduce_rows(self.cube, gather_rows(self.cube, grad, work))
+        return total, jax.tree.map(lambda *t: sum(t), *weights)
 
 
 class Buckets:
@@ -323,10 +329,13 @@
         longest = jnp.argmax(lens)
         start = ends[longest] - lens[longest]
         starts.append(start)
-        position = (jnp.arange(rows, dtype=jnp.int32) + start + rows * shard) % block_rows
-        segment = jnp.sum((position[:, None] >= ends[None, :]).astype(jnp.int32), axis=1)
-        allowed = (segment[:, None] == segment[None, :]) & (position[None, :] <= position[:, None])
-        masks.append(allowed.astype(f32))
+        both = []
+        for side in (shard, 1 - shard):
+            position = (jnp.arange(rows, dtype=jnp.int32) + start + rows * side) % block_rows
+            segment = jnp.sum((position[:, None] >= ends[None, :]).astype(jnp.int32), axis=1)
+            allowed = (segment[:, None] == segment[None, :]) & (position[None, :] <= position[:, None])
+            both.append(allowed.astype(f32))
+        masks.append(both)
 
     def turned(array, m, count=rows):
         doubled = jnp.concatenate([array, array], axis=0)
@@ -337,7 +346,9 @@
         return jax.tree.map(lambda a, b: jnp.where(first, a, b), here, there)
 
     zero_rows = jnp.zeros((rows, model), bf16)
-    token_rows = [jnp.where(first, turned(tokens[m], m), zero_rows) for m in range(micros)]
+    token_rows = [
+        jnp.where(first, turned(tokens[m], m, block_rows), jnp.zeros_like(tokens[m])) for m in range(micros)
+    ]
     cot_rows = [jnp.where(first, zero_rows, turned(cotangent[m], m)) for m in range(micros)]
 
     qkv_own = jnp.concatenate([q_weight[0], key_projection[0], value_projection[0]], axis=1)
@@ -364,69 +375,83 @@
     states, outs = [], []
     arriving = zero_rows
     for slot in range(micros + 1):
-        fresh = token_rows[slot] if slot < micros else zero_rows
-        inputs = wide(fresh + arriving)
-        allowed = pick(masks, slot)
-        hidden, normed_two, projected, heads = attention_forward(
-            inputs, allowed, gain_one, gain_two, qkv_w, out_w
-        )
+        allowed = pick(masks, slot)[0]
+        if slot == 0:
+            inputs, others = wide(token_rows[0][:rows]), wide(token_rows[0][rows:])
+            hidden, qkv, heads = head_group(normed_rows(inputs, gain_one), allowed, qkv_own, out_own)
+            sent = head_group(normed_rows(others, gain_one), pick(masks, 0)[1], qkv_own, out_own)
+            arrived = [swap(t.astype(bf16), cube.z) for t in sent]
+            hidden = inputs + hidden + wide(arrived[0])
+            groups = [(qkv, heads), tuple(arrived[1:])]
+        else:
+            fresh = token_rows[slot][:rows] if slot < micros else zero_rows
+            inputs = wide(fresh + arriving)
+            normed = normed_rows(inputs, gain_one)
+            parts = [head_group(normed, allowed, w, w_out) for w, w_out in zip(qkv_w, out_w)]
+            hidden = inputs + sum(p[0] for p in parts)
+            groups = [p[1:] for p in parts]
         table = pick(mixture.tables, slot)
-        total, saved = mixture.forward(normed_two, table)
+        total, saved = mixture.forward(normed_rows(hidden, gain_two), table)
         result = (hidden + total).astype(bf16)
         if slot < micros:
             arriving = lax.ppermute(result, "section", [(0, 1)])
         outs.append(result)
-        states.append((inputs, hidden, allowed, projected, heads, table, saved))
+        states.append((inputs, hidden, allowed, groups, table, saved))
 
     expert_sums = None
     coming = zero_rows
     attn_factors, gain_sums, input_grads = [], [], []
     for turn in range(micros + 1):
-        inputs, hidden, allowed, projected, heads, table, saved = states[micros - turn]
-        grad = coming + (cot_rows[micros - 1 - turn] if turn < micros else zero_rows)
+        sources = [turn - 1, turn + 1]
+        sources = [i if 0 <= i <= micros else None for i in sources]
+        if sources[0] is None or sources[1] is None:
+            state = states[sources[1] if sources[0] is None else sources[0]]
+        else:
+            state = jax.tree.map(
+                lambda a, b: jnp.where(first, a, b), states[sources[0]], states[sources[1]]
+            )
+        inputs, hidden, allowed, groups, table, saved = state
+        grad = coming + (cot_rows[turn] if turn < micros else zero_rows)
         grad_two, weight_grads = mixture.backward(grad, table, saved)
         expert_sums = (
             weight_grads if expert_sums is None else jax.tree.map(jnp.add, expert_sums, weight_grads)
         )
         grad_input, grad_low, normed, grads, attn_g, mlp_g = attention_backward(
-            wide(grad), grad_two, inputs, hidden, allowed, gain_one, gain_two, projected, qkv_w, out_w
+            wide(grad), grad_two, inputs, hidden, allowed, gain_one, gain_two,
+            [g[0] for g in groups], qkv_w, out_w,
         )
         if turn < micros:
             coming = lax.ppermute(grad_input.astype(bf16), "section", [(1, 0)])
-        attn_factors.append((normed, grad_low, grads, heads))
+        attn_factors.append((normed, grad_low, grads, [g[1] for g in groups]))
         gain_sums.append(jnp.concatenate([attn_g, mlp_g], axis=0))
         input_grads.append(grad_input)
 
     normed_t = jnp.concatenate([f[0] for f in attn_factors], axis=0).T
     grad_t = jnp.concatenate([f[1] for f in attn_factors], axis=0).T
-    full = []
-    for g in range(shards):
-        grad_qkv = jnp.concatenate([f[2][g] for f in attn_factors], axis=0)
-        head_rows = jnp.concatenate([f[3][g] for f in attn_factors], axis=0)
-        both = jnp.concatenate([dot_nn(normed_t, grad_qkv), dot_nn(grad_t, head_rows)], axis=1)
-        full.append(both.astype(bf16).reshape(peers, model // peers, -1))
-
-    def weight_group(group):
-        blocks = []
-        for m, s in group:
-            block = jnp.take(full[s], me ^ (m ^ cube.inner), axis=0)
-            blocks.append(block.reshape(-1, block.shape[2]))
-        return jnp.concatenate(blocks, axis=0)
-
-    total = reduce_rows(
-        cube,
-        weight_group(cube.near),
-        weight_group(cube.mate(cube.near)),
-        weight_group(cube.far),
-        weight_group(cube.mate(cube.far)),
+    share = model // peers
+
+    def owned(left, rights):
+        full = [dot_nn(left, right).astype(bf16).reshape(peers, share, -1) for right in rights]
+
+        def blocks(group):
+            taken = [jnp.take(full[s], me ^ (m ^ cube.inner), axis=0) for m, s in group]
+            return jnp.concatenate(taken, axis=0).reshape(-1, rights[0].shape[1])
+
+        return reduce_rows(cube, [tuple(blocks(group) for group in pair) for pair in cube.stages])
+
+    grad_o = owned(
+        grad_t, [jnp.concatenate([f[3][g] for f in attn_factors], axis=0) for g in range(shards)]
+    )
+    total = owned(
+        normed_t, [jnp.concatenate([f[2][g] for f in attn_factors], axis=0) for g in range(shards)]
     )
     width = q_weight.shape[2]
     grad_q = total[:, :width]
     grad_k = total[:, width : width + HEAD_SIZE]
-    grad_v = total[:, width + HEAD_SIZE : width + 2 * HEAD_SIZE]
-    grad_o = total[:, width + 2 * HEAD_SIZE :]
-    gain_total = lax.psum(sum(gain_sums), ("dp", "shard"))
-    share = model // peers
+    grad_v = total[:, width + HEAD_SIZE :]
+    gain_total = sum(gain_sums)
+    for direction in [*cube.extra, cube.core, cube.x, cube.y, cube.z]:
+        gain_total = gain_total + swap(gain_total, direction)
     gain_total = lax.dynamic_slice_in_dim(gain_total, me * share, share, 1)
 
     def placed(own, m):
@@ -445,7 +470,7 @@
     )
     input_grad = jnp.stack(
         [
-            placed(jnp.where(first, input_grads[micros - m], input_grads[micros - m - 1]), m)
+            placed(jnp.where(first, input_grads[m + 1], input_grads[m]), m)
             for m in range(micros)
         ]
     )

time: 902 us -> 809 us (0.90)
  waiting for transfers between devices: 292 us -> 195 us
  blocking collectives: 95.4 us -> 0 us
  starting transfers between devices: 148 us -> 195 us
  local copies, waits for them, and re-layouts: 71.6 us -> 94.7 us
  matrix products: 198 us -> 214 us
    psum x1 -> x0, blocking collectives: 66.9 us -> none  [local(): gain_total = lax.psum(sum(gain_sums), ('dp', 'shard'))]
    ppermute x161 -> x191, starting transfers between devices: 135 us -> 181 us  [swap(): lax.ppermute(value, axis, [(i, i ^ bit) for i in range(lax.axis_size(axis...]
    all_gather x2, waiting for transfers between devices: 40 us -> 0.01 us  [other_half(): return lax.all_gather(swap(piece, cube.z), 'dp', axis=0, tiled=True)]
    ppermute x161 -> x191, waiting for transfers between devices: 215 us -> 179 us  [swap(): lax.ppermute(value, axis, [(i, i ^ bit) for i in range(lax.axis_size(axis...]
    all_gather x1 -> x0, blocking collectives: 28.5 us -> none  [__init__(): everyone = lax.all_gather(table, ('dp', 'shard'), axis=0)]
    unnamed x625 -> x707, local copies, waits for them, and re-layouts: 44.2 us -> 58.8 us
    ppermute x2, waiting for transfers between devices: 25.1 us -> 13.3 us  [local(): coming = lax.ppermute(grad_input.astype(bf16), 'section', [(1, 0)])]
    dot_general x42 -> x53, matrix products: 64.8 us -> 75.5 us  [dot_nt(): lax.dot_general(a, b, (((1,), (1,)), ((), ())), preferred_element_type=f32)]
  transfers between devices with their start and end apart: 167 -> 197, of which waited for: 94 -> 86; matrix products, arithmetic and copies ran while one was open for 29% -> 40% of each run, Pallas kernels for 0% -> 0%
where the time goes in v2:
time: 809 us; the launch traced here: 799 us
  matrix products  214 us (26%)
  starting transfers between devices  195 us (24%)
  waiting for transfers between devices  195 us (24%)
  local copies, waits for them, and re-layouts  94.7 us (12%)
  other arithmetic  73.3 us (9%)
  between operations  26.6 us (3%)
    ppermute x191, starting transfers between devices, swap(): lax.ppermute(value, axis, [(i, i ^ bit) for i in range(lax.axis_size(axis...  181 us
    ppermute x191, waiting for transfers between devices, swap(): lax.ppermute(value, axis, [(i, i ^ bit) for i in range(lax.axis_size(axis...  179 us
    dot_general x53, matrix products, dot_nt(): lax.dot_general(a, b, (((1,), (1,)), ((), ())), preferred_element_type=f32)  75.5 us
    dot_general x39, matrix products, dot_tn(): lax.dot_general(a, b, (((0,), (0,)), ((), ())), preferred_element_type=f32)  74.8 us
    dot_general x55, matrix products, dot_nn(): lax.dot_general(a, b, (((1,), (0,)), ((), ())), preferred_element_type=f32)  64.1 us
    unnamed x707, local copies, waits for them, and re-layouts  58.8 us
  transfers between devices with their start and end apart: 197, of which 86 were waited for; matrix products, arithmetic and copies ran while one was open for 40% of the time, Pallas kernels for 0%

profile of v2, /device:TPU:0, one launch (start us, length us, event | category | flops | bytes accessed | tf_op | source)
XLA Modules:
  0.0 798.6 jit_solution(6777436552391178203)
XLA Ops:
  117.6 4.7 collective-permute-done.18
  148.4 5.9 collective-permute-done.22
  162.6 9.9 %collective-permute-done.32 = bf16[192,768]{1,0:T(8,128)(2,1)} collective-permute-done((bf16[192,768]{1,0:T(8,128)(2,1)S(1)}, bf16[192,768]{1,0:T(8,128)(2,1)}, u32[]{:S(2)}, u32[]{:S(2)}) %collective-permute-start.32) | collective-permute-done | bytes 294944 | tf_op jit(solution)/shard_map/ppermute | solution.py:55
  184.0 4.5 collective-permute-start.30
  214.5 8.7 %collective-permute-start.37 = (bf16[128,1536]{1,0:T(8,128)(2,1)S(1)}, bf16[128,1536]{1,0:T(8,128)(2,1)S(1)}, u32[]{:S(2)}, u32[]{:S(2)}) collective-permute-start(bf16[128,1536]{1,0:T(8,128)(2,1)S(1)} %get-tuple-element.144), channel_id=1, source_target_pairs={{0,1},{1,0},{2,3},{3,2},{4,5},{5,4},{6,7},{7,6},{8,9},{9,8},{10,11... | collective-permute-start | bytes 1179656 | tf_op jit(solution)/shard_map/ppermute | solution.py:55
  225.9 4.6 collective-permute-start.89
  312.3 5.4 collective-permute-done.50
  331.2 4.8 collective-permute-done.106
  337.9 8.6 %collective-permute-done.57 = bf16[128,1536]{1,0:T(8,128)(2,1)S(1)} collective-permute-done((bf16[128,1536]{1,0:T(8,128)(2,1)S(1)}, bf16[128,1536]{1,0:T(8,128)(2,1)S(1)}, u32[]{:S(2)}, u32[]{:S(2)}) %collective-permute-start.57) | collective-permute-done | bytes 393248 | tf_op jit(solution)/shard_map/ppermute | solution.py:55
  350.8 4.7 collective-permute-done.110
  355.6 5.3 collective-permute-start.59
  393.1 4.3 collective-permute-done.111
  479.4 4.2 fusion.70
  493.3 4.6 fusion.4
  498.0 4.2 fusion.277
  502.2 6.9 fusion.1
  527.0 7.3 collective-permute-done.77
  550.0 6.0 collective-permute-done.84
  582.4 9.0 %collective-permute-done.139 = bf16[128,1536]{1,0:T(8,128)(2,1)S(1)} collective-permute-done((bf16[128,1536]{1,0:T(8,128)(2,1)S(1)}, bf16[128,1536]{1,0:T(8,128)(2,1)S(1)}, u32[]{:S(2)}, u32[]{:S(2)}) %collective-permute-start.139) | collective-permute-done | bytes 393248 | tf_op jit(solution)/shard_map/ppermute | solution.py:424
  636.0 4.4 fusion.78
  655.5 6.8 fusion.13
  677.8 5.7 collective-permute-done.157
  740.1 4.3 collective-permute-done.186
  759.0 4.4 collective-permute-done.187
  (1505 shorter events, 632.7 us)
Async XLA Ops:
  7.2 193.5 %all-gather.3.cloned.1.call-start = ((), (), s32[]{:S(2)}) async-start(), calls=%async_computation | async-start | bytes 3538944 | tf_op jit(solution)/shard_map/all_gather | solution.py:360
  36.3 34.4 %collective-permute-start = (bf16[128,1536]{1,0:T(8,128)(2,1)}, bf16[128,1536]{1,0:T(8,128)(2,1)}, u32[]{:S(2)}, u32[]{:S(2)}) collective-permute-start(bf16[128,1536]{1,0:T(8,128)(2,1)} %convolution_convert_fusion.4), channel_id=1, source_target_pairs={{0,1},{1,0},{2,3},{3,2},{4,5},{5,4},{6,7},{7,6},{8,9},{9,8},{10,11... | collective-permute-start | bytes 1179656 | tf_op jit(solution)/shard_map/ppermute | solution.py:55
  44.3 47.5 %collective-permute-start.31 = (bf16[192,1024]{1,0:T(8,128)(2,1)}, bf16[192,1024]{1,0:T(8,128)(2,1)}, u32[]{:S(2)}, u32[]{:S(2)}) collective-permute-start(bf16[192,1024]{1,0:T(8,128)(2,1)} %constant_dynamic-slice_fusion.12), channel_id=1, source_target_pairs={{0,1},{1,0},{2,3},{3,2},{4,5},{5,4},{6,7},{7,6},{8,9},{9,8},{10,11... | collective-permute-start | bytes 1179656 | tf_op jit(solution)/shard_map/ppermute | solution.py:55
  91.8 116.7 %all-gather.5.cloned.1.call-start = ((), (), s32[]{:S(2)}) async-start(), calls=%async_computation.1 | async-start | bytes 2654208 | tf_op jit(solution)/shard_map/all_gather | solution.py:360
  138.2 35.3 %collective-permute-start.86 = (bf16[128,1536]{1,0:T(8,128)(2,1)}, bf16[128,1536]{1,0:T(8,128)(2,1)}, u32[]{:S(2)}, u32[]{:S(2)}) collective-permute-start(bf16[128,1536]{1,0:T(8,128)(2,1)} %get-tuple-element.138), channel_id=1, source_target_pairs={{0,4},{2,6},{4,0},{6,2},{8,12},{10,14},{12,8},{14,10},{1,5},{3,7},... | collective-permute-start | bytes 1179656 | tf_op jit(solution)/shard_map/ppermute | solution.py:55
  175.8 48.4 %collective-permute-start.92 = (bf16[128,1536]{1,0:T(8,128)(2,1)}, bf16[128,1536]{1,0:T(8,128)(2,1)}, u32[]{:S(2)}, u32[]{:S(2)}) collective-permute-start(bf16[128,1536]{1,0:T(8,128)(2,1)} %get-tuple-element.138), channel_id=1, source_target_pairs={{0,2},{2,0},{4,6},{6,4},{8,10},{10,8},{12,14},{14,12},{1,3},{3,1},... | collective-permute-start | bytes 1179656 | tf_op jit(solution)/shard_map/ppermute | solution.py:55
  178.2 53.8 %collective-permute-start.93 = (bf16[384,1536]{1,0:T(8,128)(2,1)}, bf16[384,1536]{1,0:T(8,128)(2,1)}, u32[]{:S(2)}, u32[]{:S(2)}) collective-permute-start(bf16[384,1536]{1,0:T(8,128)(2,1)} %pad_maximum_fusion.8), channel_id=1, source_target_pairs={{0,2},{2,0},{4,6},{6,4},{8,10},{10,8},{12,14},{14,12},{1,3},{3,1},... | collective-permute-start | bytes 3538952 | tf_op jit(solution)/shard_map/ppermute | solution.py:55
  224.2 33.7 %collective-permute-start.87 = (bf16[128,1536]{1,0:T(8,128)(2,1)}, bf16[128,1536]{1,0:T(8,128)(2,1)S(1)}, u32[]{:S(2)}, u32[]{:S(2)}) collective-permute-start(bf16[128,1536]{1,0:T(8,128)(2,1)} %collective-permute-done.86), channel_id=1, source_target_pairs={{0,8},{2,10},{4,12},{6,14},{8,0},{10,2},{12,4},{14,6},{1,9},{3,11}... | collective-permute-start | bytes 1179656 | tf_op jit(solution)/shard_map/ppermute | solution.py:55
  225.9 33.4 %collective-permute-start.89 = (bf16[128,1536]{1,0:T(8,128)(2,1)}, bf16[128,1536]{1,0:T(8,128)(2,1)S(1)}, u32[]{:S(2)}, u32[]{:S(2)}) collective-permute-start(bf16[128,1536]{1,0:T(8,128)(2,1)} %collective-permute-done.88), channel_id=1, source_target_pairs={{0,1},{1,0},{2,3},{3,2},{4,5},{5,4},{6,7},{7,6},{8,9},{9,8},{10,11... | collective-permute-start | bytes 1179656 | tf_op jit(solution)/shard_map/ppermute | solution.py:55
  259.6 51.7 %collective-permute-start.41 = (bf16[512,1536]{1,0:T(8,128)(2,1)S(1)}, bf16[512,1536]{1,0:T(8,128)(2,1)S(1)}, u32[]{:S(2)}, u32[]{:S(2)}) collective-permute-start(bf16[512,1536]{1,0:T(8,128)(2,1)S(1)} %get-tuple-element.53), channel_id=1, source_target_pairs={{0,2},{2,0},{4,6},{6,4},{8,10},{10,8},{12,14},{14,12},{1,3},{3,1},... | collective-permute-start | bytes 4718600 | tf_op jit(solution)/shard_map/ppermute | solution.py:55
  311.3 74.5 %collective-permute-start.137 = (bf16[128,1024]{1,0:T(8,128)(2,1)S(1)}, bf16[128,1024]{1,0:T(8,128)(2,1)S(1)}, u32[]{:S(2)}, u32[]{:S(2)}) collective-permute-start(bf16[128,1024]{1,0:T(8,128)(2,1)S(1)} %copy-done.106), channel_id=1, source_target_pairs={{0,1},{1,0},{2,3},{3,2},{4,5},{5,4},{6,7},{7,6},{8,9},{9,8},{10,11... | collective-permute-start | bytes 786440 | tf_op jit(solution)/shard_map/ppermute | solution.py:55
  323.4 77.0 %collective-permute-start.182 = (bf16[128,768]{0,1:T(8,128)(2,1)S(1)}, bf16[128,768]{0,1:T(8,128)(2,1)S(1)}, u32[]{:S(2)}, u32[]{:S(2)}) collective-permute-start(bf16[128,768]{0,1:T(8,128)(2,1)S(1)} %copy-done.152), channel_id=1, source_target_pairs={{0,1},{1,0},{2,3},{3,2},{4,5},{5,4},{6,7},{7,6},{8,9},{9,8},{10,11... | collective-permute-start | bytes 589832 | tf_op jit(solution)/shard_map/ppermute | solution.py:55
  448.9 77.0 %collective-permute-start.68 = (bf16[512,1536]{1,0:T(8,128)(2,1)}, bf16[512,1536]{1,0:T(8,128)(2,1)}, u32[]{:S(2)}, u32[]{:S(2)}) collective-permute-start(bf16[512,1536]{1,0:T(8,128)(2,1)} %get-tuple-element.58), channel_id=1, source_target_pairs={{0,2},{2,0},{4,6},{6,4},{8,10},{10,8},{12,14},{14,12},{1,3},{3,1},... | collective-permute-start | bytes 4718600 | tf_op jit(solution)/shard_map/ppermute | solution.py:55
  468.3 40.8 %collective-permute-start.82 = (bf16[32,1536]{1,0:T(8,128)(2,1)S(1)}, bf16[32,1536]{1,0:T(8,128)(2,1)S(1)}, u32[]{:S(2)}, u32[]{:S(2)}) collective-permute-start(bf16[32,1536]{1,0:T(8,128)(2,1)S(1)} %slice.1969), channel_id=1, source_target_pairs={{0,8},{2,10},{4,12},{6,14},{8,0},{10,2},{12,4},{14,6},{1,9},{3,11}... | collective-permute-start | bytes 294920 | tf_op jit(solution)/shard_map/ppermute | solution.py:55
  469.4 41.0 %collective-permute-start.134 = (bf16[32,1536]{1,0:T(8,128)(2,1)S(1)}, bf16[32,1536]{1,0:T(8,128)(2,1)S(1)}, u32[]{:S(2)}, u32[]{:S(2)}) collective-permute-start(bf16[32,1536]{1,0:T(8,128)(2,1)S(1)} %slice.2029), channel_id=1, source_target_pairs={{0,8},{2,10},{4,12},{6,14},{8,0},{10,2},{12,4},{14,6},{1,9},{3,11}... | collective-permute-start | bytes 294920 | tf_op jit(solution)/shard_map/ppermute | solution.py:55
  478.0 39.7 %collective-permute-start.70 = (bf16[384,1536]{1,0:T(8,128)(2,1)}, bf16[384,1536]{1,0:T(8,128)(2,1)}, u32[]{:S(2)}, u32[]{:S(2)}) collective-permute-start(bf16[384,1536]{1,0:T(8,128)(2,1)} %slice.1957), channel_id=1, source_target_pairs={{0,2},{2,0},{4,6},{6,4},{8,10},{10,8},{12,14},{14,12},{1,3},{3,1},... | collective-permute-start | bytes 3538952 | tf_op jit(solution)/shard_map/ppermute | solution.py:55
  558.2 35.0 %collective-permute-start.85 = (bf16[128,768]{1,0:T(8,128)(2,1)S(1)}, bf16[128,768]{1,0:T(8,128)(2,1)S(1)}, u32[]{:S(2)}, u32[]{:S(2)}) collective-permute-start(bf16[128,768]{1,0:T(8,128)(2,1)S(1)} %constant_dynamic-slice_fusion.9), channel_id=1, source_target_pairs={{0,1},{1,0},{2,3},{3,2},{4,5},{5,4},{6,7},{7,6},{8,9},{9,8},{10,11... | collective-permute-start | bytes 589832 | tf_op jit(solution)/shard_map/ppermute | solution.py:55
  580.3 37.7 %collective-permute-start.138 = (f32[128,768]{1,0:T(8,128)S(1)}, f32[128,768]{1,0:T(8,128)S(1)}, u32[]{:S(2)}, u32[]{:S(2)}) collective-permute-start(f32[128,768]{1,0:T(8,128)S(1)} %constant_dynamic-slice_fusion.7), channel_id=1, source_target_pairs={{0,1},{1,0},{2,3},{3,2},{4,5},{5,4},{6,7},{7,6},{8,9},{9,8},{10,11... | collective-permute-start | bytes 1179656 | tf_op jit(solution)/shard_map/ppermute | solution.py:55
  623.7 54.0 %collective-permute-start.148 = (bf16[512,1536]{1,0:T(8,128)(2,1)}, bf16[512,1536]{1,0:T(8,128)(2,1)}, u32[]{:S(2)}, u32[]{:S(2)}) collective-permute-start(bf16[512,1536]{1,0:T(8,128)(2,1)} %get-tuple-element.73), channel_id=1, source_target_pairs={{0,2},{2,0},{4,6},{6,4},{8,10},{10,8},{12,14},{14,12},{1,3},{3,1},... | collective-permute-start | bytes 4718600 | tf_op jit(solution)/shard_map/ppermute | solution.py:55
  632.3 39.4 %collective-permute-start.156 = (bf16[48,1536]{1,0:T(8,128)(2,1)}, bf16[48,1536]{1,0:T(8,128)(2,1)}, u32[]{:S(2)}, u32[]{:S(2)}) collective-permute-start(bf16[48,1536]{1,0:T(8,128)(2,1)} %get-tuple-element.259), channel_id=1, source_target_pairs={{0,1},{1,0},{2,3},{3,2},{4,5},{5,4},{6,7},{7,6},{8,9},{9,8},{10,11... | collective-permute-start | bytes 442376 | tf_op jit(solution)/shard_map/ppermute | solution.py:55
  634.1 37.6 %collective-permute-start.162 = (bf16[32,1536]{1,0:T(8,128)(2,1)}, bf16[32,1536]{1,0:T(8,128)(2,1)}, u32[]{:S(2)}, u32[]{:S(2)}) collective-permute-start(bf16[32,1536]{1,0:T(8,128)(2,1)} %slice.2087), channel_id=1, source_target_pairs={{0,8},{2,10},{4,12},{6,14},{8,0},{10,2},{12,4},{14,6},{1,9},{3,11}... | collective-permute-start | bytes 294920 | tf_op jit(solution)/shard_map/ppermute | solution.py:55
  635.1 36.6 %collective-permute-start.159 = (bf16[48,1536]{1,0:T(8,128)(2,1)}, bf16[48,1536]{1,0:T(8,128)(2,1)}, u32[]{:S(2)}, u32[]{:S(2)}) collective-permute-start(bf16[48,1536]{1,0:T(8,128)(2,1)} %get-tuple-element.260), channel_id=1, source_target_pairs={{0,4},{2,6},{4,0},{6,2},{8,12},{10,14},{12,8},{14,10},{1,5},{3,7},... | collective-permute-start | bytes 442376 | tf_op jit(solution)/shard_map/ppermute | solution.py:55
  715.7 40.9 %collective-permute-start.171 = (bf16[576,1024]{1,0:T(8,128)(2,1)S(1)}, bf16[576,1024]{1,0:T(8,128)(2,1)S(1)}, u32[]{:S(2)}, u32[]{:S(2)}) collective-permute-start(bf16[576,1024]{1,0:T(8,128)(2,1)S(1)} %bitcast.651), channel_id=1, source_target_pairs={{0,2},{2,0},{4,6},{6,4},{8,10},{10,8},{12,14},{14,12},{1,3},{3,1},... | collective-permute-start | bytes 3538952 | tf_op jit(solution)/shard_map/ppermute | solution.py:55
  736.0 38.9 %collective-permute-start.170 = (bf16[768,1024]{1,0:T(8,128)(2,1)S(1)}, bf16[768,1024]{1,0:T(8,128)(2,1)S(1)}, u32[]{:S(2)}, u32[]{:S(2)}) collective-permute-start(bf16[768,1024]{1,0:T(8,128)(2,1)S(1)} %bitcast.650), channel_id=1, source_target_pairs={{0,2},{2,0},{4,6},{6,4},{8,10},{10,8},{12,14},{14,12},{1,3},{3,1},... | collective-permute-start | bytes 4718600 | tf_op jit(solution)/shard_map/ppermute | solution.py:55
  (432 other events, 3434.4 us)
Sparse Core Ops, SparseCore 0:
  91.9 36.5 all-gather.2
  175.9 28.7 all-gather.4

commit v3 on v2

--- a/solution.py
+++ b/solution.py
@@ -1,7 +1,11 @@
+import functools
+
 import jax
 import jax.numpy as jnp
 import numpy as np
 from jax import lax
+from jax.experimental import pallas as pl
+from jax.experimental.pallas import tpu as pltpu
 from jax.sharding import PartitionSpec as P
 
 HEAD_SIZE = 128
@@ -66,17 +70,17 @@
     near = [swap(own, d) for d in (cube.x, cube.y, cube.z)]
     own_mate = swap(own, cube.core)
     middle = [swap(block, d) for block, d in zip(near, (cube.y, cube.z, cube.x))]
-    near_mate = swap(jnp.concatenate(near, axis=0), cube.core)
-    done = [work(0, [own, *near, own_mate, near_mate])]
+    near_mate = [swap(block, cube.core) for block in near]
+    done = [work(0, [own, *near, own_mate, *near_mate])]
     middle, done = lax.optimization_barrier((middle, done))
     cuts = thirds(own.shape[0])
     last = [
         swap(block[lo:hi], d) for block, d, (lo, hi) in zip(middle, (cube.z, cube.x, cube.y), cuts)
     ]
-    middle_mate = swap(jnp.concatenate(middle, axis=0), cube.core)
-    done.append(work(1, [*middle, middle_mate]))
-    last = jnp.concatenate(last, axis=0)
-    done.append(work(2, [last, swap(last, cube.core)]))
+    middle_mate = [swap(block, cube.core) for block in middle]
+    done.append(work(1, [*middle, *middle_mate]))
+    last_mate = [swap(block, cube.core) for block in last]
+    done.append(work(2, [*last, *last_mate]))
     return done
 
 
@@ -153,32 +157,232 @@
     return dot_nt(head_out, w_out), qkv, head_out
 
 
-def attention_backward(grad, grad_two, inputs, hidden, allowed, attn_gain, mlp_gain, projected, qkv_w, out_w):
+VMEM = pl.BlockSpec(memory_space=pltpu.VMEM)
+SMEM = pl.BlockSpec(memory_space=pltpu.SMEM)
+MIB = 1 << 20
+
+
+def like(shape, dtype):
+    return jax.ShapeDtypeStruct(shape, dtype)
+
+
+def on_device(body, outs, args, flops, mib, scalars=()):
+    moved = sum(a.size * a.dtype.itemsize for a in [*args, *outs])
+    return pl.pallas_call(
+        body,
+        out_shape=outs,
+        in_specs=[SMEM] * len(scalars) + [VMEM] * len(args),
+        out_specs=[VMEM] * len(outs),
+        compiler_params=pltpu.CompilerParams(vmem_limit_bytes=mib * MIB),
+        cost_estimate=pl.CostEstimate(flops=flops, bytes_accessed=moved, transcendentals=0),
+    )(*scalars, *args)
+
+
+def half_heads_body(inputs, others, mask, other_mask, gain, w, w_out, *outs):
+    for rows, allowed, (part, qkv, heads) in (
+        (inputs, mask, outs[:3]),
+        (others, other_mask, outs[3:]),
+    ):
+        normed = normed_rows(wide(rows[...]), gain[...])
+        value, qkv[...], heads[...] = head_group(normed, allowed[...], w[...], w_out[...])
+        part[...] = value.astype(part.dtype)
+
+
+def half_heads(inputs, others, mask, other_mask, gain, w, w_out):
+    rows, model = inputs.shape
+    shapes = [
+        like((rows, model), f32), like((rows, w.shape[1]), bf16), like((rows, w_out.shape[1]), bf16),
+        like((rows, model), bf16), like((rows, w.shape[1]), bf16), like((rows, w_out.shape[1]), bf16),
+    ]
+    args = [inputs, others, mask, other_mask, gain, w, w_out]
+    return on_device(half_heads_body, shapes, args, 4 * rows * (w.size + w_out.size), 32)
+
+
+def joined_body(inputs, own, other, gain, extra, hidden, payload):
+    total = wide(inputs[...]) + own[...] + wide(other[...])
+    hidden[...] = total
+    model = total.shape[1]
+    payload[:, :model] = normed_rows(total, gain[...])
+    payload[:, model:] = extra[...]
+
+
+def joined(inputs, own, other, gain, extra):
+    rows, model = inputs.shape
+    shapes = [like((rows, model), f32), like((rows, model + extra.shape[1]), bf16)]
+    return on_device(joined_body, shapes, [inputs, own, other, gain, extra], 10 * rows * model, 16)
+
+
+def attention_body(fresh, arriving, mask, gain, gain_two, extra, w0, w1, o0, o1, *outs):
+    inputs, hidden, payload, qkv0, qkv1, heads0, heads1 = outs
+    rows = fresh[...] + arriving[...]
+    inputs[...] = rows
+    total = wide(rows)
+    normed = normed_rows(total, gain[...])
+    for w, w_out, qkv, heads in ((w0, o0, qkv0, heads0), (w1, o1, qkv1, heads1)):
+        value, qkv[...], heads[...] = head_group(normed, mask[...], w[...], w_out[...])
+        total = total + value
+    hidden[...] = total
+    model = total.shape[1]
+    payload[:, :model] = normed_rows(total, gain_two[...])
+    payload[:, model:] = extra[...]
+
+
+def attention_forward(fresh, arriving, mask, gain, gain_two, extra, qkv_w, out_w):
+    rows, model = fresh.shape
+    w, w_out = qkv_w[0], out_w[0]
+    shapes = [
+        like((rows, model), bf16), like((rows, model), f32), like((rows, model + extra.shape[1]), bf16),
+        like((rows, w.shape[1]), bf16), like((rows, w.shape[1]), bf16),
+        like((rows, w_out.shape[1]), bf16), like((rows, w_out.shape[1]), bf16),
+    ]
+    args = [fresh, arriving, mask, gain, gain_two, extra, *qkv_w, *out_w]
+    outs = on_device(attention_body, shapes, args, 4 * rows * (w.size + w_out.size), 40)
+    inputs, hidden, payload, qkv0, qkv1, heads0, heads1 = outs
+    return inputs, hidden, payload, [(qkv0, heads0), (qkv1, heads1)]
+
+
+def attention_back_body(grad, grad_two, inputs, hidden, mask, gain, gain_two, q0, q1, w0, w1, o0, o1, *outs):
+    grad_input, grad_input_low, grad_low, normed, g0, g1, gain_grad, gain_two_grad = outs
     rows = inputs.shape[0]
-    normed = (inputs * norm_factor(inputs) * attn_gain).astype(bf16)
-    back, mlp_gain_grad = norm_back(hidden, norm_factor(hidden), mlp_gain, grad_two)
-    grad_hidden = grad + back
-    grad_low = grad_hidden.astype(bf16)
-    grad_normed = 0.0
-    grads = []
-    for qkv, w, w_out in zip(projected, qkv_w, out_w):
+    values = wide(inputs[...])
+    normed[...] = normed_rows(values, gain[...])
+    total = hidden[...]
+    back, gain_two_grad[...] = norm_back(total, norm_factor(total), gain_two[...], grad_two[...])
+    grad_hidden = wide(grad[...]) + back
+    low = grad_hidden.astype(bf16)
+    grad_low[...] = low
+    grad_normed = jnp.zeros_like(grad_hidden)
+    for qkv_ref, w, w_out, grad_qkv in ((q0, w0, o0, g0), (q1, w1, o1, g1)):
+        qkv = qkv_ref[...]
         width = qkv.shape[1] - 2 * HEAD_SIZE
-        grad_heads = stack_heads(dot_nn(grad_low, w_out).astype(bf16))
+        grad_heads = stack_heads(dot_nn(low, w_out[...]).astype(bf16))
         query = stack_heads(qkv[:, :width])
         key, value = qkv[:, width : width + HEAD_SIZE], qkv[:, width + HEAD_SIZE :]
-        tiled = jnp.concatenate([allowed] * (width // HEAD_SIZE), axis=0)
+        tiled = jnp.concatenate([mask[...]] * (width // HEAD_SIZE), axis=0)
         probs = head_probs(query, key, tiled)
         grad_probs = dot_nt(grad_heads, value)
         inner = jnp.sum(probs * grad_probs, axis=1, keepdims=True)
         grad_scores = (probs * (grad_probs - inner) * HEAD_SIZE ** (-0.5)).astype(bf16)
-        grad_query = spread_heads(dot_nn(grad_scores, key).astype(bf16), rows)
-        grad_key = dot_tn(grad_scores, query).astype(bf16)
-        grad_value = dot_tn(probs.astype(bf16), grad_heads).astype(bf16)
-        grad_qkv = jnp.concatenate([grad_query, grad_key, grad_value], axis=1)
-        grad_normed = grad_normed + dot_nt(grad_qkv, w)
-        grads.append(grad_qkv)
-    back, attn_gain_grad = norm_back(inputs, norm_factor(inputs), attn_gain, grad_normed)
-    return grad_hidden + back, grad_low, normed, grads, attn_gain_grad, mlp_gain_grad
+        grad_qkv[:, :width] = spread_heads(dot_nn(grad_scores, key).astype(bf16), rows)
+        grad_qkv[:, width : width + HEAD_SIZE] = dot_tn(grad_scores, query).astype(bf16)
+        grad_qkv[:, width + HEAD_SIZE :] = dot_tn(probs.astype(bf16), grad_heads).astype(bf16)
+        grad_normed = grad_normed + dot_nt(grad_qkv[...], w[...])
+    back, gain_grad[...] = norm_back(values, norm_factor(values), gain[...], grad_normed)
+    result = grad_hidden + back
+    grad_input[...] = result
+    grad_input_low[...] = result.astype(bf16)
+
+
+def attention_backward(grad, grad_two, inputs, hidden, mask, gain, gain_two, projected, qkv_w, out_w):
+    rows, model = inputs.shape
+    w, w_out = qkv_w[0], out_w[0]
+    shapes = [
+        like((rows, model), f32), like((rows, model), bf16), like((rows, model), bf16),
+        like((rows, model), bf16), like((rows, w.shape[1]), bf16), like((rows, w.shape[1]), bf16),
+        like((1, model), f32), like((1, model), f32),
+    ]
+    args = [grad, grad_two, inputs, hidden, mask, gain, gain_two, *projected, *qkv_w, *out_w]
+    return on_device(attention_back_body, shapes, args, 4 * rows * (w.size + w_out.size), 40)
+
+
+def place(pieces, *targets):
+    at = 0
+    for piece in pieces:
+        rows, first = piece.shape[0], 0
+        for target in targets:
+            target[at : at + rows, :] = piece[:, first : first + target.shape[1]]
+            first += target.shape[1]
+        at += rows
+
+
+def own_gate(extra, me, peers):
+    lane = lax.broadcasted_iota(jnp.int32, extra.shape, 1)
+    return jnp.sum(jnp.where((lane == me) | (lane == me + peers), wide(extra), 0.0), axis=1, keepdims=True)
+
+
+def chunked(rows, step):
+    count = max(c for c in (128, 192, 256, 384) if rows % c == 0)
+    if rows == count:
+        step(0, count)
+    else:
+        pl.loop(0, rows // count)(lambda i: step(pl.multiple_of(i * count, count), count))
+
+
+def expert_stage_body(peers, pieces, me_ref, *refs):
+    ins, (rows, extra, gate_out, up_out, *parts) = refs[:pieces], refs[pieces + 3 :]
+    w_gate, w_up, w_down = refs[pieces : pieces + 3]
+    me = me_ref[0]
+    place(ins, rows, extra)
+    half = rows.shape[0] // 2
+    for i, part in enumerate(parts):
+
+        def step(first, count, i=i, part=part):
+            here = pl.ds(first + i * half, count)
+            values = rows[here, :]
+            gate = dot_nn(values, w_gate[...])
+            up = dot_nn(values, w_up[...])
+            gate_out[here, :] = gate.astype(bf16)
+            up_out[here, :] = up.astype(bf16)
+            act = (gate / (1.0 + jnp.exp(-gate)) * up).astype(bf16)
+            scale = own_gate(extra[here, :], me, peers)
+            part[pl.ds(first, count), :] = (scale * dot_nn(act, w_down[...])).astype(bf16)
+
+        chunked(half, step)
+
+
+def expert_stage(pieces, me, peers, w_gate, w_up, w_down):
+    count = sum(p.shape[0] for p in pieces)
+    model, units = w_gate.shape
+    shapes = [
+        like((count, model), bf16), like((count, pieces[0].shape[1] - model), bf16),
+        like((count, units), bf16), like((count, units), bf16),
+        like((count // 2, model), bf16), like((count // 2, model), bf16),
+    ]
+    body = functools.partial(expert_stage_body, peers, len(pieces))
+    outs = on_device(body, shapes, [*pieces, w_gate, w_up, w_down], 6 * count * w_gate.size, 40, (me,))
+    return outs[4:], outs[:4]
+
+
+def expert_back_body(peers, pieces, me_ref, *refs):
+    ins = refs[:pieces]
+    extra, gate_in, up_in, w_gate, w_up, w_down, grad_rows, grad_gate, grad_up, act, *parts = refs[pieces:]
+    me = me_ref[0]
+    place(ins, grad_rows)
+    half = grad_rows.shape[0] // 2
+    for i, part in enumerate(parts):
+
+        def step(first, count, i=i, part=part):
+            here = pl.ds(first + i * half, count)
+            scale = own_gate(extra[here, :], me, peers)
+            scaled = (scale * wide(grad_rows[here, :])).astype(bf16)
+            grad_rows[here, :] = scaled
+            grad_act = dot_nt(scaled, w_down[...])
+            gate, up = wide(gate_in[here, :]), wide(up_in[here, :])
+            sig = 1.0 / (1.0 + jnp.exp(-gate))
+            silu = gate * sig
+            low_gate = (grad_act * up * sig * (1.0 + gate * (1.0 - sig))).astype(bf16)
+            low_up = (grad_act * silu).astype(bf16)
+            grad_gate[here, :] = low_gate
+            grad_up[here, :] = low_up
+            act[here, :] = (silu * up).astype(bf16)
+            grad_in = dot_nt(low_gate, w_gate[...]) + dot_nt(low_up, w_up[...])
+            part[pl.ds(first, count), :] = grad_in.astype(bf16)
+
+        chunked(half, step)
+
+
+def expert_back_stage(pieces, me, peers, saved, w_gate, w_up, w_down):
+    rows, extra, gate_out, up_out = saved
+    count = rows.shape[0]
+    model, units = w_gate.shape
+    shapes = [
+        like((count, model), bf16), like((count, units), bf16), like((count, units), bf16),
+        like((count, units), bf16), like((count // 2, model), bf16), like((count // 2, model), bf16),
+    ]
+    body = functools.partial(expert_back_body, peers, len(pieces))
+    args = [*pieces, extra, gate_out, up_out, w_gate, w_up, w_down]
+    outs = on_device(body, shapes, args, 6 * count * w_gate.size, 40, (me,))
+    return outs[4:], outs[:4]
 
 
 def expert_forward(pieces, gate_col, w_gate, w_up, w_down):
@@ -216,49 +420,37 @@
 class Blocks:
     def __init__(self, cube, routes, gates, weights):
         self.cube, self.weights = cube, weights
-        micros = routes.shape[0]
-        peers = lax.axis_size("dp")
+        self.peers = lax.axis_size("dp")
+        self.me = lax.axis_index("dp").astype(jnp.int32).reshape(1)
         rows = routes.shape[1] // lax.axis_size("shard")
-        numbers = jnp.arange(peers, dtype=jnp.int32)[:, None, None]
-        table = jnp.concatenate(
-            [
-                jnp.sum(jnp.where(routes[m, :rows].T == numbers, gates[m, :rows].T, 0.0), axis=1)
-                for m in range(micros)
-            ],
-            axis=0,
+        numbers = jnp.arange(self.peers, dtype=jnp.int32)
+        table = jnp.sum(
+            jnp.where(routes[:, :rows, :, None] == numbers, gates[:, :rows, :, None], 0.0), axis=2
         )
-        places = [(0, 0)]
-        for axis, bit in [*cube.extra, cube.core, cube.x, cube.y, cube.z]:
-            table = jnp.concatenate([table, swap(table, (axis, bit))], axis=1)
-            places += [(m | bit, s) if axis == "dp" else (m, s | bit) for m, s in places]
-        mine = [
-            lax.dynamic_index_in_dim(table, m * peers + lax.axis_index("dp"), 0, keepdims=False)
-            for m in range(micros)
-        ]
-
-        def ordered(values, groups):
-            order = [places.index((m ^ int(i), s)) for group in groups for m, s in group for i in cube.inner]
-            return jnp.concatenate([values[p * rows : (p + 1) * rows] for p in order]).reshape(-1, 1)
-
-        self.tables = [[ordered(values, groups) for groups in cube.stages] for values in mine]
-
-    def forward(self, own, table):
+        high = lax.reduce_precision(table, 8, 7)
+        both = jnp.concatenate([high, table - high], axis=2).astype(bf16)
+        self.extras = jnp.pad(both, ((0, 0), (0, 0), (0, 128 - both.shape[2])))
+        self.tables = [()] * routes.shape[0]
+
+    def forward(self, payload, table):
         saved = []
 
         def work(stage, pieces):
-            part, kept = expert_forward(pieces, table[stage], *self.weights)
+            parts, kept = expert_stage(pieces, self.me, self.peers, *self.weights)
             saved.append(kept)
-            return halves(part)
-
-        return reduce_rows(self.cube, gather_rows(self.cube, own, work)), saved
+            return parts
+
+        return reduce_rows(self.cube, gather_rows(self.cube, payload, work)), saved
 
     def backward(self, grad, table, saved):
         weights = []
 
         def work(stage, pieces):
-            grad_in, weight_grads = expert_backward(pieces, table[stage], saved[stage], *self.weights)
-            weights.append(weight_grads)
-            return halves(grad_in)
+            parts, kept = expert_back_stage(pieces, self.me, self.peers, saved[stage], *self.weights)
+            grad_rows, grad_gate, grad_up, act = kept
+            rows = saved[stage][0]
+            weights.append((dot_tn(rows, grad_gate), dot_tn(rows, grad_up), dot_tn(act, grad_rows)))
+            return parts
 
         total = reduce_rows(self.cube, gather_rows(self.cube, grad, work))
         return total, jax.tree.map(lambda *t: sum(t), *weights)
@@ -269,6 +461,7 @@
         self.cube, self.weights, self.capacity = cube, weights, capacity
         micros, self.rows, self.top = routes.shape
         self.experts = lax.axis_size("dp")
+        self.extras = jnp.zeros((micros, self.rows // lax.axis_size("shard"), 128), bf16)
         self.tables = []
         for m in range(micros):
             flat = routes[m].reshape(-1)
@@ -293,6 +486,7 @@
 
     def forward(self, own, table):
         target, source, gates = table
+        own = own[:, : own.shape[1] - self.extras.shape[2]]
         padded = jnp.pad(self.whole(own), ((0, 1), (0, 0)))
         arrived = self.exchange(jnp.take(padded, source // self.top, axis=0))
         part, saved = expert_forward([arrived], None, *self.weights)
@@ -376,22 +570,22 @@
     arriving = zero_rows
     for slot in range(micros + 1):
         allowed = pick(masks, slot)[0]
+        extra = pick(mixture.extras, slot)
         if slot == 0:
-            inputs, others = wide(token_rows[0][:rows]), wide(token_rows[0][rows:])
-            hidden, qkv, heads = head_group(normed_rows(inputs, gain_one), allowed, qkv_own, out_own)
-            sent = head_group(normed_rows(others, gain_one), pick(masks, 0)[1], qkv_own, out_own)
-            arrived = [swap(t.astype(bf16), cube.z) for t in sent]
-            hidden = inputs + hidden + wide(arrived[0])
+            inputs, others = token_rows[0][:rows], token_rows[0][rows:]
+            own, qkv, heads, *sent = half_heads(
+                inputs, others, allowed, pick(masks, 0)[1], gain_one, qkv_own, out_own
+            )
+            arrived = [swap(t, cube.z) for t in sent]
+            hidden, payload = joined(inputs, own, arrived[0], gain_two, extra)
             groups = [(qkv, heads), tuple(arrived[1:])]
         else:
             fresh = token_rows[slot][:rows] if slot < micros else zero_rows
-            inputs = wide(fresh + arriving)
-            normed = normed_rows(inputs, gain_one)
-            parts = [head_group(normed, allowed, w, w_out) for w, w_out in zip(qkv_w, out_w)]
-            hidden = inputs + sum(p[0] for p in parts)
-            groups = [p[1:] for p in parts]
+            inputs, hidden, payload, groups = attention_forward(
+                fresh, arriving, allowed, gain_one, gain_two, extra, qkv_w, out_w
+            )
         table = pick(mixture.tables, slot)
-        total, saved = mixture.forward(normed_rows(hidden, gain_two), table)
+        total, saved = mixture.forward(payload, table)
         result = (hidden + total).astype(bf16)
         if slot < micros:
             arriving = lax.ppermute(result, "section", [(0, 1)])
@@ -416,12 +610,11 @@
         expert_sums = (
             weight_grads if expert_sums is None else jax.tree.map(jnp.add, expert_sums, weight_grads)
         )
-        grad_input, grad_low, normed, grads, attn_g, mlp_g = attention_backward(
-            wide(grad), grad_two, inputs, hidden, allowed, gain_one, gain_two,
-            [g[0] for g in groups], qkv_w, out_w,
+        grad_input, sent, grad_low, normed, *grads, attn_g, mlp_g = attention_backward(
+            grad, grad_two, inputs, hidden, allowed, gain_one, gain_two, [g[0] for g in groups], qkv_w, out_w
         )
         if turn < micros:
-            coming = lax.ppermute(grad_input.astype(bf16), "section", [(1, 0)])
+            coming = lax.ppermute(sent, "section", [(1, 0)])
         attn_factors.append((normed, grad_low, grads, [g[1] for g in groups]))
         gain_sums.append(jnp.concatenate([attn_g, mlp_g], axis=0))
         input_grads.append(grad_input)

time: 809 us -> 799 us (0.988)
  Pallas kernels: 0 us -> 135 us
  matrix products: 214 us -> 88.8 us
  waiting for transfers between devices: 195 us -> 217 us
  other arithmetic: 73.3 us -> 56.2 us
  starting transfers between devices: 195 us -> 182 us
    pallas_call x0 -> x25, Pallas kernels: none -> 135 us  [on_device(): pl.pallas_call(body, out_shape=outs, in_specs=[SMEM] * len(scalars) + [VM...]
    dot_general x53 -> x0, matrix products: 75.5 us -> none  [dot_nt(): lax.dot_general(a, b, (((1,), (1,)), ((), ())), preferred_element_type=f32)]
    dot_general x55 -> x4, matrix products: 64.1 us -> 6.75 us  [dot_nn(): lax.dot_general(a, b, (((1,), (0,)), ((), ())), preferred_element_type=f32)]
    ppermute x191 -> x223, waiting for transfers between devices: 179 us -> 201 us  [swap(): lax.ppermute(value, axis, [(i, i ^ bit) for i in range(lax.axis_size(axis...]
    ppermute x191 -> x223, starting transfers between devices: 181 us -> 168 us  [swap(): lax.ppermute(value, axis, [(i, i ^ bit) for i in range(lax.axis_size(axis...]
    concatenate x26 -> x1, other arithmetic: 10.9 us -> 0.6 us  [__init__(): both = jnp.concatenate([high, table - high], axis=2).astype(bf16)]
    slice x18 -> x2, local copies, waits for them, and re-layouts: 9.05 us -> 0.08 us  [the longest x1 0.05 us: local(): inputs, others = (token_rows[0][:rows], token_rows[0][rows:])]
    dot_general x39 -> x27, matrix products: 74.8 us -> 82 us  [dot_tn(): lax.dot_general(a, b, (((0,), (0,)), ((), ())), preferred_element_type=f32)]
  transfers between devices with their start and end apart: 197 -> 229, of which waited for: 86 -> 83; matrix products, arithmetic and copies ran while one was open for 40% -> 21% of each run, Pallas kernels for 0% -> 16%
where the time goes in v3:
time: 799 us; the launch traced here: 790 us
  waiting for transfers between devices  217 us (27%)
  starting transfers between devices  182 us (23%)
  Pallas kernels  135 us (17%)
  local copies, waits for them, and re-layouts  88.9 us (11%)
  matrix products  88.8 us (11%)
  other arithmetic  56.2 us (7%)
  between operations  23.7 us (3%)
    ppermute x223, waiting for transfers between devices, swap(): lax.ppermute(value, axis, [(i, i ^ bit) for i in range(lax.axis_size(axis...  201 us
    ppermute x223, starting transfers between devices, swap(): lax.ppermute(value, axis, [(i, i ^ bit) for i in range(lax.axis_size(axis...  168 us
    pallas_call x25, Pallas kernels, on_device(): pl.pallas_call(body, out_shape=outs, in_specs=[SMEM] * len(scalars) + [VM...  135 us
    dot_general x27, matrix products, dot_tn(): lax.dot_general(a, b, (((0,), (0,)), ((), ())), preferred_element_type=f32)  82 us
    unnamed x496, local copies, waits for them, and re-layouts  64.7 us
    convert_element_type x24, other arithmetic, low_sum(): return sum((wide(t) for t in terms)).astype(bf16)  17.6 us
  transfers between devices with their start and end apart: 229, of which 83 were waited for; matrix products, arithmetic and copies ran while one was open for 21% of the time, Pallas kernels for 16%

profile of v3, /device:TPU:0, one launch (start us, length us, event | category | flops | bytes accessed | tf_op | source)
XLA Modules:
  0.0 790.5 jit_solution(9744295425021853834)
XLA Ops:
  55.9 7.2 collective-permute-done.1.refs_1_
  65.6 9.2 %collective-permute-done.33 = bf16[192,1024]{1,0:T(8,128)(2,1)S(1)} collective-permute-done((bf16[192,1024]{1,0:T(8,128)(2,1)S(1)}, bf16[192,1024]{1,0:T(8,128)(2,1)S(1)}, u32[]{:S(2)}, u32[]{:S(2)}) %collective-permute-start.33) | collective-permute-done | bytes 393248 | tf_op jit(solution)/shard_map/ppermute | solution.py:59
  82.5 9.6 %shard_map.511 = (bf16[1024,1536]{1,0:T(8,128)(2,1)}, bf16[1024,128]{1,0:T(8,128)(2,1)S(1)}, bf16[1024,384]{1,0:T(8,128)(2,1)S(1)}, bf16[1024,384]{1,0:T(8,128)(...) custom-call(s32[1]{0:T(128)} %bitcast.23.me_ref, bf16[128,1664]{1,0:T(8,128)(2,1)} %get-tuple-element.203.refs_0_, ...), custom_call_target="tpu_custom_call" | custom-call | flops 3623878656 | bytes 15073280 | tf_op jit(solution)/shard_map/pallas_call | solution.py:171
  177.3 9.6 %collective-permute-start.39 = (bf16[128,1664]{1,0:T(8,128)(2,1)S(1)}, bf16[128,1664]{1,0:T(8,128)(2,1)S(1)}, u32[]{:S(2)}, u32[]{:S(2)}) collective-permute-start(bf16[128,1664]{1,0:T(8,128)(2,1)S(1)} %get-tuple-element.216.refs_0_), channel_id=1, source_target_pairs={{0,1},{1,0},{2,3},{3,2},{4,5},{5,4},{6,7},{7,6},{8,9},{9,8},{10,11... | collective-permute-start | bytes 1277960 | tf_op jit(solution)/shard_map/ppermute | solution.py:59
  189.5 6.6 collective-permute-done.39.refs_3_
  204.2 7.4 shard_map.515
  214.0 9.9 %shard_map.522 = (bf16[1024,1536]{1,0:T(8,128)(2,1)}, bf16[1024,384]{1,0:T(8,128)(2,1)S(1)}, bf16[1024,384]{1,0:T(8,128)(2,1)S(1)}, bf16[1024,384]{1,0:T(8,128)(...) custom-call(s32[1]{0:T(128)} %bitcast.23.me_ref, bf16[128,1536]{1,0:T(8,128)(2,1)} %fusion.96.refs_0_.grad, ...), custom_call_target="tpu_custom_call" | custom-call | flops 3623878656 | bytes 17170432 | tf_op jit(solution)/shard_map/pallas_call | solution.py:171
  272.9 5.6 shard_map.523
  328.9 7.7 collective-permute-done.126
  337.9 7.1 collective-permute-done.65
  348.2 5.8 collective-permute-start.67
  355.5 6.4 shard_map.525
  383.6 8.9 %collective-permute-done.132.refs_1_ = bf16[128,1536]{1,0:T(8,128)(2,1)} collective-permute-done((bf16[128,1536]{1,0:T(8,128)(2,1)S(1)}, bf16[128,1536]{1,0:T(8,128)(2,1)}, u32[]{:S(2)}, u32[]{:S(2)}) %collective-permute-start.132) | collective-permute-done | bytes 393248 | tf_op jit(solution)/shard_map/ppermute | solution.py:59
  397.0 7.8 shard_map.519
  427.5 9.7 %shard_map.526 = (bf16[1024,1536]{1,0:T(8,128)(2,1)}, bf16[1024,384]{1,0:T(8,128)(2,1)S(1)}, bf16[1024,384]{1,0:T(8,128)(2,1)S(1)}, bf16[1024,384]{1,0:T(8,128)(...) custom-call(s32[1]{0:T(128)} %bitcast.23.me_ref, bf16[128,1536]{1,0:T(8,128)(2,1)S(1)} %fusion.94.refs_0_.grad, ...), custom_call_target="tpu_custom_call" | custom-call | flops 3623878656 | bytes 17170432 | tf_op jit(solution)/shard_map/pallas_call | solution.py:171
  477.8 5.9 shard_map.527
  502.1 5.8 fusion.9
  539.8 6.7 collective-permute-done.155
  568.2 6.5 shard_map.529
  576.0 6.3 fusion.15
  582.3 7.2 collective-permute-done.165.refs_0_.grad
  612.0 9.8 %shard_map.530 = (bf16[1024,1536]{1,0:T(8,128)(2,1)}, bf16[1024,384]{1,0:T(8,128)(2,1)S(1)}, bf16[1024,384]{1,0:T(8,128)(2,1)S(1)}, bf16[1024,384]{1,0:T(8,128)(...) custom-call(s32[1]{0:T(128)} %bitcast.23.me_ref, ...), custom_call_target="tpu_custom_call" | custom-call | flops 3623878656 | bytes 17170432 | tf_op jit(solution)/shard_map/pallas_call | solution.py:171
  689.6 7.2 shard_map.533
  762.1 6.5 collective-permute-done.206
  (1142 shorter events, 586.4 us)
Async XLA Ops:
  7.2 155.1 %all-gather.5.cloned.1.call-start = ((), (), s32[]{:S(2)}) async-start(), calls=%async_computation.1 | async-start | bytes 2654208 | tf_op jit(solution)/shard_map/all_gather | solution.py:554
  25.7 136.6 %all-gather.3.cloned.1.call-start = ((), (), s32[]{:S(2)}) async-start(), calls=%async_computation | async-start | bytes 3538944 | tf_op jit(solution)/shard_map/all_gather | solution.py:554
  139.5 37.2 %collective-permute-start.102 = (bf16[128,1536]{1,0:T(8,128)(2,1)}, bf16[128,1536]{1,0:T(8,128)(2,1)}, u32[]{:S(2)}, u32[]{:S(2)}) collective-permute-start(bf16[128,1536]{1,0:T(8,128)(2,1)} %fusion.96.refs_0_.grad), channel_id=1, source_target_pairs={{0,8},{2,10},{4,12},{6,14},{8,0},{10,2},{12,4},{14,6},{1,9},{3,11}... | collective-permute-start | bytes 1179656 | tf_op jit(solution)/shard_map/ppermute | solution.py:59
  143.8 33.5 %collective-permute-start.104 = (bf16[128,1536]{1,0:T(8,128)(2,1)}, bf16[128,1536]{1,0:T(8,128)(2,1)}, u32[]{:S(2)}, u32[]{:S(2)}) collective-permute-start(bf16[128,1536]{1,0:T(8,128)(2,1)} %fusion.96.refs_0_.grad), channel_id=1, source_target_pairs={{0,1},{1,0},{2,3},{3,2},{4,5},{5,4},{6,7},{7,6},{8,9},{9,8},{10,11... | collective-permute-start | bytes 1179656 | tf_op jit(solution)/shard_map/ppermute | solution.py:59
  147.8 39.2 %collective-permute-start.106 = (bf16[128,1536]{1,0:T(8,128)(2,1)}, bf16[128,1536]{1,0:T(8,128)(2,1)}, u32[]{:S(2)}, u32[]{:S(2)}) collective-permute-start(bf16[128,1536]{1,0:T(8,128)(2,1)} %fusion.96.refs_0_.grad), channel_id=1, source_target_pairs={{0,2},{2,0},{4,6},{6,4},{8,10},{10,8},{12,14},{14,12},{1,3},{3,1},... | collective-permute-start | bytes 1179656 | tf_op jit(solution)/shard_map/ppermute | solution.py:59
  154.0 33.0 %collective-permute-start.101 = (bf16[128,1536]{1,0:T(8,128)(2,1)}, bf16[128,1536]{1,0:T(8,128)(2,1)}, u32[]{:S(2)}, u32[]{:S(2)}) collective-permute-start(bf16[128,1536]{1,0:T(8,128)(2,1)} %collective-permute-done.100.refs_1_), channel_id=1, source_target_pairs={{0,8},{2,10},{4,12},{6,14},{8,0},{10,2},{12,4},{14,6},{1,9},{3,11}... | collective-permute-start | bytes 1179656 | tf_op jit(solution)/shard_map/ppermute | solution.py:59
  198.7 30.2 %collective-permute-start.103 = (bf16[128,1536]{1,0:T(8,128)(2,1)}, bf16[128,1536]{1,0:T(8,128)(2,1)S(1)}, u32[]{:S(2)}, u32[]{:S(2)}) collective-permute-start(bf16[128,1536]{1,0:T(8,128)(2,1)} %collective-permute-done.102.refs_2_), channel_id=1, source_target_pairs={{0,1},{1,0},{2,3},{3,2},{4,5},{5,4},{6,7},{7,6},{8,9},{9,8},{10,11... | collective-permute-start | bytes 1179656 | tf_op jit(solution)/shard_map/ppermute | solution.py:59
  200.7 28.2 %collective-permute-start.105 = (bf16[128,1536]{1,0:T(8,128)(2,1)}, bf16[128,1536]{1,0:T(8,128)(2,1)S(1)}, u32[]{:S(2)}, u32[]{:S(2)}) collective-permute-start(bf16[128,1536]{1,0:T(8,128)(2,1)} %collective-permute-done.104.refs_3_), channel_id=1, source_target_pairs={{0,4},{2,6},{4,0},{6,2},{8,12},{10,14},{12,8},{14,10},{1,5},{3,7},... | collective-permute-start | bytes 1179656 | tf_op jit(solution)/shard_map/ppermute | solution.py:59
  201.6 28.1 %collective-permute-start.36 = (bf16[128,1664]{1,0:T(8,128)(2,1)S(1)}, bf16[128,1664]{1,0:T(8,128)(2,1)S(1)}, u32[]{:S(2)}, u32[]{:S(2)}) collective-permute-start(bf16[128,1664]{1,0:T(8,128)(2,1)S(1)} %collective-permute-done.35.refs_1_), channel_id=1, source_target_pairs={{0,8},{2,10},{4,12},{6,14},{8,0},{10,2},{12,4},{14,6},{1,9},{3,11}... | collective-permute-start | bytes 1277960 | tf_op jit(solution)/shard_map/ppermute | solution.py:59
  263.3 48.3 %collective-permute-start.45 = (bf16[512,1536]{1,0:T(8,128)(2,1)S(1)}, bf16[512,1536]{1,0:T(8,128)(2,1)}, u32[]{:S(2)}, u32[]{:S(2)}) collective-permute-start(bf16[512,1536]{1,0:T(8,128)(2,1)S(1)} %copy-done.139), channel_id=1, source_target_pairs={{0,2},{2,0},{4,6},{6,4},{8,10},{10,8},{12,14},{14,12},{1,3},{3,1},... | collective-permute-start | bytes 4718600 | tf_op jit(solution)/shard_map/ppermute | solution.py:59
  269.6 34.4 %collective-permute-start.49 = (bf16[384,1536]{1,0:T(8,128)(2,1)S(1)}, bf16[384,1536]{1,0:T(8,128)(2,1)}, u32[]{:S(2)}, u32[]{:S(2)}) collective-permute-start(bf16[384,1536]{1,0:T(8,128)(2,1)S(1)} %get-tuple-element.225), channel_id=1, source_target_pairs={{0,2},{2,0},{4,6},{6,4},{8,10},{10,8},{12,14},{14,12},{1,3},{3,1},... | collective-permute-start | bytes 3538952 | tf_op jit(solution)/shard_map/ppermute | solution.py:59
  279.3 31.1 %collective-permute-start.114 = (bf16[384,1536]{1,0:T(8,128)(2,1)S(1)}, bf16[384,1536]{1,0:T(8,128)(2,1)S(1)}, u32[]{:S(2)}, u32[]{:S(2)}) collective-permute-start(bf16[384,1536]{1,0:T(8,128)(2,1)S(1)} %get-tuple-element.255), channel_id=1, source_target_pairs={{0,2},{2,0},{4,6},{6,4},{8,10},{10,8},{12,14},{14,12},{1,3},{3,1},... | collective-permute-start | bytes 3538952 | tf_op jit(solution)/shard_map/ppermute | solution.py:59
  311.6 69.2 %collective-permute-start.163 = (bf16[128,1024]{1,0:T(8,128)(2,1)S(1)}, bf16[128,1024]{1,0:T(8,128)(2,1)}, u32[]{:S(2)}, u32[]{:S(2)}) collective-permute-start(bf16[128,1024]{1,0:T(8,128)(2,1)S(1)} %copy-done.163), channel_id=1, source_target_pairs={{0,1},{1,0},{2,3},{3,2},{4,5},{5,4},{6,7},{7,6},{8,9},{9,8},{10,11... | collective-permute-start | bytes 786440 | tf_op jit(solution)/shard_map/ppermute | solution.py:59
  463.9 74.9 %collective-permute-start.142 = (bf16[512,1536]{1,0:T(8,128)(2,1)}, bf16[512,1536]{1,0:T(8,128)(2,1)}, u32[]{:S(2)}, u32[]{:S(2)}) collective-permute-start(bf16[512,1536]{1,0:T(8,128)(2,1)} %get-tuple-element.274), channel_id=1, source_target_pairs={{0,2},{2,0},{4,6},{6,4},{8,10},{10,8},{12,14},{14,12},{1,3},{3,1},... | collective-permute-start | bytes 4718600 | tf_op jit(solution)/shard_map/ppermute | solution.py:59
  464.0 51.4 %collective-permute-start.89 = (bf16[128,1536]{1,0:T(8,128)(2,1)S(1)}, bf16[128,1536]{1,0:T(8,128)(2,1)}, u32[]{:S(2)}, u32[]{:S(2)}) collective-permute-start(bf16[128,1536]{1,0:T(8,128)(2,1)S(1)} %get-tuple-element.240), channel_id=1, source_target_pairs={{0,2},{2,0},{4,6},{6,4},{8,10},{10,8},{12,14},{14,12},{1,3},{3,1},... | collective-permute-start | bytes 1179656 | tf_op jit(solution)/shard_map/ppermute | solution.py:59
  472.7 44.8 %collective-permute-start.153 = (bf16[128,1536]{1,0:T(8,128)(2,1)}, bf16[128,1536]{1,0:T(8,128)(2,1)}, u32[]{:S(2)}, u32[]{:S(2)}) collective-permute-start(bf16[128,1536]{1,0:T(8,128)(2,1)} %get-tuple-element.293), channel_id=1, source_target_pairs={{0,2},{2,0},{4,6},{6,4},{8,10},{10,8},{12,14},{14,12},{1,3},{3,1},... | collective-permute-start | bytes 1179656 | tf_op jit(solution)/shard_map/ppermute | solution.py:59
  473.6 62.3 %collective-permute-start.82 = (bf16[384,1536]{1,0:T(8,128)(2,1)}, bf16[384,1536]{1,0:T(8,128)(2,1)}, u32[]{:S(2)}, u32[]{:S(2)}) collective-permute-start(bf16[384,1536]{1,0:T(8,128)(2,1)} %get-tuple-element.238), channel_id=1, source_target_pairs={{0,2},{2,0},{4,6},{6,4},{8,10},{10,8},{12,14},{14,12},{1,3},{3,1},... | collective-permute-start | bytes 3538952 | tf_op jit(solution)/shard_map/ppermute | solution.py:59
  483.7 45.7 %collective-permute-start.146 = (bf16[384,1536]{1,0:T(8,128)(2,1)S(1)}, bf16[384,1536]{1,0:T(8,128)(2,1)S(1)}, u32[]{:S(2)}, u32[]{:S(2)}) collective-permute-start(bf16[384,1536]{1,0:T(8,128)(2,1)S(1)} %get-tuple-element.285), channel_id=1, source_target_pairs={{0,2},{2,0},{4,6},{6,4},{8,10},{10,8},{12,14},{14,12},{1,3},{3,1},... | collective-permute-start | bytes 3538952 | tf_op jit(solution)/shard_map/ppermute | solution.py:59
  560.5 30.7 %collective-permute-start.98 = (bf16[128,1536]{1,0:T(8,128)(2,1)}, bf16[128,1536]{1,0:T(8,128)(2,1)}, u32[]{:S(2)}, u32[]{:S(2)}) collective-permute-start(bf16[128,1536]{1,0:T(8,128)(2,1)} %get-tuple-element.435), channel_id=1, source_target_pairs={{0,1},{1,0},{2,3},{3,2},{4,5},{5,4},{6,7},{7,6},{8,9},{9,8},{10,11... | collective-permute-start | bytes 1179656 | tf_op jit(solution)/shard_map/ppermute | solution.py:59
  560.8 30.3 %collective-permute-start.95 = (bf16[128,1536]{1,0:T(8,128)(2,1)S(1)}, bf16[128,1536]{1,0:T(8,128)(2,1)}, u32[]{:S(2)}, u32[]{:S(2)}) collective-permute-start(bf16[128,1536]{1,0:T(8,128)(2,1)S(1)} %get-tuple-element.436), channel_id=1, source_target_pairs={{0,8},{2,10},{4,12},{6,14},{8,0},{10,2},{12,4},{14,6},{1,9},{3,11}... | collective-permute-start | bytes 1179656 | tf_op jit(solution)/shard_map/ppermute | solution.py:59
  632.0 40.8 %collective-permute-start.176 = (bf16[512,1536]{1,0:T(8,128)(2,1)}, bf16[512,1536]{1,0:T(8,128)(2,1)}, u32[]{:S(2)}, u32[]{:S(2)}) collective-permute-start(bf16[512,1536]{1,0:T(8,128)(2,1)} %get-tuple-element.305), channel_id=1, source_target_pairs={{0,2},{2,0},{4,6},{6,4},{8,10},{10,8},{12,14},{14,12},{1,3},{3,1},... | collective-permute-start | bytes 4718600 | tf_op jit(solution)/shard_map/ppermute | solution.py:59
  703.8 46.0 %collective-permute-start.203 = (bf16[576,1024]{1,0:T(8,128)(2,1)S(1)}, bf16[576,1024]{1,0:T(8,128)(2,1)S(1)}, u32[]{:S(2)}, u32[]{:S(2)}) collective-permute-start(bf16[576,1024]{1,0:T(8,128)(2,1)S(1)} %bitcast.336), channel_id=1, source_target_pairs={{0,2},{2,0},{4,6},{6,4},{8,10},{10,8},{12,14},{14,12},{1,3},{3,1},... | collective-permute-start | bytes 3538952 | tf_op jit(solution)/shard_map/ppermute | solution.py:59
  722.4 47.9 %collective-permute-start.202 = (bf16[768,1024]{1,0:T(8,128)(2,1)S(1)}, bf16[768,1024]{1,0:T(8,128)(2,1)S(1)}, u32[]{:S(2)}, u32[]{:S(2)}) collective-permute-start(bf16[768,1024]{1,0:T(8,128)(2,1)S(1)} %bitcast.335), channel_id=1, source_target_pairs={{0,2},{2,0},{4,6},{6,4},{8,10},{10,8},{12,14},{14,12},{1,3},{3,1},... | collective-permute-start | bytes 4718600 | tf_op jit(solution)/shard_map/ppermute | solution.py:59
  722.5 35.8 %collective-permute-start.215 = (bf16[768,768]{1,0:T(8,128)(2,1)S(1)}, bf16[768,768]{1,0:T(8,128)(2,1)S(1)}, u32[]{:S(2)}, u32[]{:S(2)}) collective-permute-start(bf16[768,768]{1,0:T(8,128)(2,1)S(1)} %bitcast.337), channel_id=1, source_target_pairs={{0,2},{2,0},{4,6},{6,4},{8,10},{10,8},{12,14},{14,12},{1,3},{3,1},... | collective-permute-start | bytes 3538952 | tf_op jit(solution)/shard_map/ppermute | solution.py:59
  (451 other events, 4148.1 us)
Sparse Core Ops, SparseCore 0:
  25.8 29.2 all-gather.4
  78.8 32.8 all-gather.2
